TPU v7x, 32 devices: a whole 2x2x4 slice. The times are simulated.
32 devices in a mesh: dp: 2 (over core), row: 4 (over y, x), col: 4 (over z).
Axes of the slice: x: 2, y: 2, z: 4, core: 2. Of those that a mesh axis runs over, the one named last changes fastest.
Arguments:
- features: bfloat16 [64, 48, 2048], P(('dp', 'row'), 'col'), parts along dimension 0, may hold values from 0 to 40
- low_level: bfloat16 [128, 96, 256], P(('dp', 'row'), 'col'), parts along dimension 0, may hold values from -6 to 6
- point_weight: bfloat16 [2048, 256], P(None, 'row'), may hold values from -0.125 to 0.125
- atrous_weight: bfloat16 [3, 3, 3, 2048, 256], P(None, None, None, None, 'row'), may hold values from -0.046875 to 0.046875
- pool_weight: bfloat16 [2048, 256], P(None, 'row'), may hold values from -0.125 to 0.125
- aspp_bias: float32 [5, 256], P(None, 'row'), may hold values from -1.5 to 1.5
- proj_weight: bfloat16 [1280, 256], replicated, may hold values from -0.15625 to 0.15625
- proj_bias: float32 [256], replicated, may hold values from -1.5 to 1.5
- low_weight: bfloat16 [256, 48], replicated, may hold values from -0.375 to 0.375
- low_bias: float32 [48], replicated, may hold values from -1.5 to 1.5
- conv1_weight: bfloat16 [3, 3, 304, 256], replicated, may hold values from -0.109375 to 0.109375
- conv1_bias: float32 [256], replicated, may hold values from -1.5 to 1.5
- conv2_weight: bfloat16 [3, 3, 256, 256], replicated, may hold values from -0.125 to 0.125
- conv2_bias: float32 [256], replicated, may hold values from -1.5 to 1.5
Outputs:
- decoded: bfloat16 [128, 96, 256], P(('dp', 'row'), 'col'), parts along dimension 0
There are 2 independent parts, one for each index of `dp`. A program takes and returns all parts, laid end to end along the dimension named above; an argument that names none is the same for every part. Nothing has to cross between parts.
All inputs are finite; a program needn't handle non-finite values.
Results may differ from a plain program's by a relative error of at most 0.0057.
Values may be sent and summed in bfloat16 or wider, within the bound.
A program may use at most 128 MiB of HBM per device.

v0:
```python
import jax
import jax.numpy as jnp
from jax import lax
from jax.sharding import PartitionSpec as P

RATES = (12, 24, 36)


def from_behind(value, axis, by):
    devices = lax.axis_size(axis)
    pairs = [(i, i + by) for i in range(devices) if 0 <= i + by < devices]
    return lax.ppermute(value, axis, pairs)


def padded_2(value, sides, width):
    for axis, dim in sides:
        devices, length = (lax.axis_size(axis), value.shape[dim])
        up = [(i, (i + 1) % devices) for i in range(devices - 1)]
        down = [(j, i) for i, j in up]
        last = lax.slice_in_dim(value, length - width, length, axis=dim)
        first = lax.slice_in_dim(value, 0, width, axis=dim)
        before = lax.ppermute(last, axis, up)
        after = lax.ppermute(first, axis, down)
        value = jnp.concatenate([before, value, after], axis=dim)
    return value


def enlarge(padded):
    values = padded.astype(jnp.float32)
    middle = values[1:-1]
    even = 0.75 * middle + 0.25 * values[:-2]
    odd = 0.75 * middle + 0.25 * values[2:]
    values = jnp.stack([even, odd], axis=1).reshape(
        2 * middle.shape[0], middle.shape[1], middle.shape[2]
    )
    middle = values[:, 1:-1]
    even = 0.75 * middle + 0.25 * values[:, :-2]
    odd = 0.75 * middle + 0.25 * values[:, 2:]
    values = jnp.stack([even, odd], axis=2).reshape(
        values.shape[0], 2 * middle.shape[1], middle.shape[2]
    )
    return values.astype(jnp.bfloat16)


def convolve(padded, weight, bias):
    height, width = (padded.shape[0] - 2, padded.shape[1] - 2)
    windows = []
    for row_tap in range(3):
        for col_tap in range(3):
            windows.append(padded[row_tap : row_tap + height, col_tap : col_tap + width])
    columns = jnp.concatenate(windows, axis=2)
    depth = columns.shape[2]
    result = jnp.dot(
        columns.reshape(-1, depth), weight.reshape(depth, -1), preferred_element_type=jnp.float32
    )
    result = jnp.maximum(result + bias, 0.0).astype(jnp.bfloat16)
    return result.reshape(height, width, -1)


def local_rows(values, offset):
    height = values.shape[0]
    if abs(offset) >= height:
        return jnp.zeros_like(values)
    extent = abs(offset)
    padded = jnp.pad(values, ((extent, extent), (0, 0), (0, 0)))
    return padded[extent + offset : extent + offset + height]


def bring_cols(values, steps):
    if steps == 0:
        return values
    return from_behind(values, "col", steps)


def move_cols(values, distance):
    width = values.shape[1]
    whole = distance // width
    pieces = bring_cols(values, -whole)
    return pieces


def fix_edges(padded, at_start, at_end, axis_number):
    size = padded.shape[axis_number]
    first = lax.slice_in_dim(padded, 0, 1, axis=axis_number)
    second = lax.slice_in_dim(padded, 1, 2, axis=axis_number)
    middle = lax.slice_in_dim(padded, 1, size - 1, axis=axis_number)
    before = lax.slice_in_dim(padded, size - 2, size - 1, axis=axis_number)
    final = lax.slice_in_dim(padded, size - 1, size, axis=axis_number)
    first = jnp.where(at_start, second, first)
    final = jnp.where(at_end, before, final)
    return jnp.concatenate([first, middle, final], axis=axis_number)


def on_device(
    features,
    low_level,
    point_weight,
    atrous_weight,
    pool_weight,
    aspp_bias,
    proj_weight,
    proj_bias,
    low_weight,
    low_bias,
    conv1_weight,
    conv1_bias,
    conv2_weight,
    conv2_bias,
):
    in_width = features.shape[2]
    own_width = point_weight.shape[1]
    out_width = proj_weight.shape[1]
    row_count = lax.axis_size("row")
    col_count = lax.axis_size("col")
    row_index = lax.axis_index("row")
    col_index = lax.axis_index("col")
    tile_rows, tile_cols = (features.shape[0], features.shape[1])
    full_rows = tile_rows * row_count
    full_cols = tile_cols * col_count
    atrous_flat = jnp.transpose(atrous_weight.reshape(27, in_width, own_width), (1, 0, 2)).reshape(
        in_width, 27 * own_width
    )
    own_stack = jnp.concatenate([point_weight, atrous_flat, pool_weight], axis=1)
    group_total = 28
    stacked = own_stack[:, : group_total * own_width]
    piece = lax.all_gather(features, "row", axis=0, tiled=True)
    result = jnp.dot(piece.reshape(-1, in_width), stacked, preferred_element_type=jnp.float32)
    products = result.reshape(piece.shape[0], piece.shape[1], -1)
    map_rows = products.shape[0]

    def group(number):
        return products[:, :, number * own_width : (number + 1) * own_width]

    all_width = own_width * row_count
    first_col = jnp.where(col_index == 0, 1.0, 0.0).astype(jnp.float32)
    spread_bias = lax.dynamic_update_slice_in_dim(
        jnp.zeros((5, all_width), jnp.float32), aspp_bias * first_col, row_index * own_width, 1
    )
    tile_sum = jnp.sum(features.astype(jnp.float32), axis=(0, 1))
    scene_sum, full_bias = lax.psum((tile_sum, spread_bias), ("row", "col"))
    pooled = jnp.dot(
        scene_sum, pool_weight.astype(jnp.float32), precision=lax.Precision.HIGHEST
    ) / (full_rows * full_cols)
    last_axis = full_bias.ndim - 1
    bias_mine = lax.dynamic_slice_in_dim(full_bias, row_index * own_width, own_width, last_axis)

    def activate(values, number):
        return jnp.maximum(values + bias_mine[number], 0.0).astype(jnp.bfloat16)

    outputs = [activate(group(0), 0)]
    for rate_number in range(3):
        dilation = RATES[rate_number]
        running = jnp.zeros((map_rows, tile_cols, own_width), jnp.float32)
        for col_tap in range(3):
            column_sum = jnp.zeros((map_rows, tile_cols, own_width), jnp.float32)
            for row_tap in range(3):
                row_values = group(1 + rate_number * 9 + row_tap * 3 + col_tap)
                offset = (row_tap - 1) * RATES[rate_number]
                column_sum = column_sum + local_rows(row_values, offset)
            running = running + move_cols(column_sum, (col_tap - 1) * dilation)
        outputs.append(activate(running, rate_number + 1))
    pool_branch = jnp.maximum(pooled + bias_mine[4], 0.0).astype(jnp.bfloat16)
    outputs.append(jnp.broadcast_to(pool_branch, (map_rows, tile_cols, own_width)))
    branches = jnp.concatenate(outputs, axis=2)
    blocks = proj_weight.reshape(5, row_count, own_width, out_width)
    swapped = lax.all_to_all(branches, "row", split_axis=0, concat_axis=2, tiled=True)
    reordered = jnp.transpose(blocks, (1, 0, 2, 3)).reshape(-1, out_width)
    summed = jnp.dot(
        swapped.reshape(-1, swapped.shape[2]), reordered, preferred_element_type=jnp.float32
    )
    coarse = (
        jnp.maximum(summed + proj_bias, 0.0)
        .astype(jnp.bfloat16)
        .reshape(tile_rows, tile_cols, out_width)
    )
    padded = padded_2(coarse, (("row", 0), ("col", 1)), 1)
    padded = fix_edges(padded, row_index == 0, row_index == row_count - 1, 0)
    padded = fix_edges(padded, col_index == 0, col_index == col_count - 1, 1)
    upsampled = enlarge(padded)
    low_rows = low_level.reshape(-1, low_level.shape[2])
    reduced = jnp.dot(low_rows, low_weight, preferred_element_type=jnp.float32)
    reduced = (
        jnp.maximum(reduced + low_bias, 0.0)
        .astype(jnp.bfloat16)
        .reshape(low_level.shape[0], low_level.shape[1], -1)
    )
    joined_fine = jnp.concatenate([upsampled, reduced], axis=2)
    padded_fine = padded_2(joined_fine, (("row", 0), ("col", 1)), 1)
    hidden = convolve(padded_fine, conv1_weight, conv1_bias)
    padded_hidden = padded_2(hidden, (("row", 0), ("col", 1)), 1)
    return convolve(padded_hidden, conv2_weight, conv2_bias)


def solution(mesh):
    placed = (
        P(("dp", "row"), "col", None),
        P(("dp", "row"), "col", None),
        P(None, "row"),
        P(None, None, None, None, "row"),
        P(None, "row"),
        P(None, "row"),
        P(),
        P(),
        P(),
        P(),
        P(),
        P(),
        P(),
        P(),
    )
    return jax.shard_map(
        on_device,
        mesh=mesh,
        in_specs=placed,
        out_specs=P(("dp", "row"), "col", None),
        check_vma=False,
    )
```

profile of v0, /device:TPU:0, one launch (start us, length us, event | category | flops | bytes accessed | tf_op | source)
XLA Modules:
  0.0 230.5 jit_solution(14696281862383564626)
XLA Ops:
  8.1 1.1 convert_reduce_fusion
  9.1 79.2 %all-reduce.12 = (f32[5,256]{1,0:T(8,128)S(1)}, f32[2048]{0:T(1024)S(1)}) all-reduce(f32[5,256]{1,0:T(8,128)S(1)} %dynamic_update_slice.3, f32[2048]{0:T(1024)S(1)} %convert_reduce_fusion), channel_id=1, replica_groups=mesh['dp'=2,'row'=4,'col'=4] {'row','col'}, use_global_device_ids=true, to_apply=%region_0.1 | all-reduce | flops 3328 | bytes 26624 | tf_op jit(solution)/shard_map/psum | solution.py:140
  88.4 2.3 copy.25
  90.7 1.4 reshape.87
  92.1 8.1 %fusion.4 = f32[384,1792]{1,0:T(8,128)} fusion(bf16[384,2048]{1,0:T(8,128)(2,1)} %reshape.87, bf16[2048,1728]{0,1:T(8,128)(2,1)} %bitcast.118, bf16[2048,64]{0,1:T(8,128)(2,1)} %param.16), kind=kOutput, calls=%fused_computation.4 | convolution fusion | flops 2833252352 | bytes 11665408 | tf_op jit(solution)/shard_map/dot_general | solution.py:127
  100.2 4.0 %reshape.88 = f32[32,12,1792]{2,1,0:T(8,128)} reshape(f32[384,1792]{1,0:T(8,128)} %fusion.4) | data formatting | bytes 5505024 | tf_op jit(solution)/shard_map/reshape | solution.py:128
  104.2 1.1 fusion.56
  105.3 1.3 collective-permute-start.4
  106.6 1.3 collective-permute-start.5
  107.9 4.5 %collective-permute-done.4 = f32[32,12,64]{2,1,0:T(8,128)S(1)} collective-permute-done((f32[32,12,64]{2,1,0:T(8,128)S(1)}, f32[32,12,64]{2,1,0:T(8,128)S(1)}, u32[]{:S(2)}, u32[]{:S(2)}) %collective-permute-start.4) | collective-permute-done | bytes 98336 | tf_op jit(solution)/shard_map/ppermute | solution.py:12
  112.5 5.3 %collective-permute-done.5 = f32[32,12,64]{2,1,0:T(8,128)S(1)} collective-permute-done((f32[32,12,64]{2,1,0:T(8,128)S(1)}, f32[32,12,64]{2,1,0:T(8,128)S(1)}, u32[]{:S(2)}, u32[]{:S(2)}) %collective-permute-start.5) | collective-permute-done | bytes 98336 | tf_op jit(solution)/shard_map/ppermute | solution.py:12
  117.7 2.7 %fusion.44 = (bf16[32,12,64]{2,1,0:T(8,128)(2,1)S(1)}, f32[32,12,64]{2,1,0:T(8,128)S(1)}, f32[32,12,64]{2,1,0:T(8,128)S(1)}, f32[32,12,64]{2,1,0:T(8,128)S(1)}, ...) fusion(f32[32,12,64]{2,1,0:T(8,128)S(1)} %collective-permute-do, ...), kind=kLoop, calls=%fused_computation.71 | loop fusion | flops 196608 | bytes 2851328 | tf_op jit(solution)/shard_map/convert_element_type | solution.py:148
  120.4 1.2 fusion.31
  121.6 1.3 collective-permute-start.2
  122.9 1.3 collective-permute-start.3
  124.2 4.5 %collective-permute-done.2 = f32[32,12,64]{2,1,0:T(8,128)S(1)} collective-permute-done((f32[32,12,64]{2,1,0:T(8,128)S(1)}, f32[32,12,64]{2,1,0:T(8,128)S(1)}, u32[]{:S(2)}, u32[]{:S(2)}) %collective-permute-start.2) | collective-permute-done | bytes 98336 | tf_op jit(solution)/shard_map/ppermute | solution.py:12
  128.7 7.1 %collective-permute-done.3 = f32[32,12,64]{2,1,0:T(8,128)S(1)} collective-permute-done((f32[32,12,64]{2,1,0:T(8,128)S(1)}, f32[32,12,64]{2,1,0:T(8,128)S(1)}, u32[]{:S(2)}, u32[]{:S(2)}) %collective-permute-start.3) | collective-permute-done | bytes 98336 | tf_op jit(solution)/shard_map/ppermute | solution.py:12
  135.8 1.3 fusion.38
  137.1 1.3 collective-permute-start
  138.5 1.3 collective-permute-start.1
  140.1 2.2 collective-permute-done
  142.3 4.4 %collective-permute-done.1 = f32[32,12,64]{2,1,0:T(8,128)S(1)} collective-permute-done((f32[32,12,64]{2,1,0:T(8,128)S(1)}, f32[32,12,64]{2,1,0:T(8,128)S(1)}, u32[]{:S(2)}, u32[]{:S(2)}) %collective-permute-start.1) | collective-permute-done | bytes 98336 | tf_op jit(solution)/shard_map/ppermute | solution.py:12
  146.7 1.1 fusion.27
  147.8 1.0 concatenate.103
  148.8 3.6 %all-to-all-start = ((bf16[32,12,320]{2,1,0:T(8,128)(2,1)}), bf16[32,12,320]{2,1,0:T(8,128)(2,1)S(1)}, u32[]{:S(2)}, u32[]{:S(2)}) async-start(bf16[32,12,320]{2,1,0:T(8,128)(2,1)} %concatenate.103), calls=%async_computation | async-start | bytes 786432 | tf_op jit(solution)/shard_map/all_to_all | solution.py:166
  152.5 5.7 %all-to-all-done = bf16[32,12,320]{2,1,0:T(8,128)(2,1)S(1)} async-done(((bf16[32,12,320]{2,1,0:T(8,128)(2,1)}), bf16[32,12,320]{2,1,0:T(8,128)(2,1)S(1)}, u32[]{:S(2)}, u32[]{:S(2)}) %all-to-all-start) | async-done | bytes 245792 | tf_op jit(solution)/shard_map/all_to_all | solution.py:166
  159.1 3.4 %collective-permute-start.6 = (bf16[1,12,256]{2,1,0:T(8,128)(2,1)S(1)}, bf16[1,12,256]{2,1,0:T(8,128)(2,1)S(1)}, u32[]{:S(2)}, u32[]{:S(2)}) collective-permute-start(bf16[1,12,256]{2,1,0:T(8,128)(2,1)S(1)} %get-tuple-element.67), channel_id=1, source_target_pairs={{0,4},{4,8},{8,12},{1,5},{5,9},{9,13},{2,6},{6,10},{10,14},{3,7},{... | collective-permute-start | bytes 18440 | tf_op jit(solution)/shard_map/ppermute | solution.py:22
  162.5 1.3 collective-permute-start.7
  163.8 4.2 %collective-permute-done.7 = bf16[1,12,256]{2,1,0:T(8,128)(2,1)S(1)} collective-permute-done((bf16[1,12,256]{2,1,0:T(8,128)(2,1)S(1)}, bf16[1,12,256]{2,1,0:T(8,128)(2,1)S(1)}, u32[]{:S(2)}, u32[]{:S(2)}) %collective-permute-start.7) | collective-permute-done | bytes 6176 | tf_op jit(solution)/shard_map/ppermute | solution.py:23
  168.0 2.6 %collective-permute-start.8 = (bf16[10,1,256]{2,1,0:T(2,128)(2,1)S(1)}, bf16[10,1,256]{2,1,0:T(2,128)(2,1)S(1)}, u32[]{:S(2)}, u32[]{:S(2)}) collective-permute-start(bf16[10,1,256]{2,1,0:T(2,128)(2,1)S(1)} %get-tuple-element.64), channel_id=1, source_target_pairs={{0,1},{1,2},{2,3},{4,5},{5,6},{6,7},{8,9},{9,10},{10,11},{12,13},{... | collective-permute-start | bytes 15368 | tf_op jit(solution)/shard_map/ppermute | solution.py:22
  170.7 1.3 collective-permute-start.9
  172.4 3.9 %collective-permute-done.9 = bf16[10,1,256]{2,1,0:T(2,128)(2,1)S(1)} collective-permute-done((bf16[10,1,256]{2,1,0:T(2,128)(2,1)S(1)}, bf16[10,1,256]{2,1,0:T(2,128)(2,1)S(1)}, u32[]{:S(2)}, u32[]{:S(2)}) %collective-permute-start.9) | collective-permute-done | bytes 5152 | tf_op jit(solution)/shard_map/ppermute | solution.py:23
  177.1 4.3 %collective-permute-start.10 = (bf16[1,24,304]{2,0,1:T(2,128)(2,1)S(1)}, bf16[1,24,304]{2,0,1:T(2,128)(2,1)S(1)}, u32[]{:S(2)}, u32[]{:S(2)}) collective-permute-start(bf16[1,24,304]{2,0,1:T(2,128)(2,1)S(1)} %get-tuple-element.46), channel_id=1, source_target_pairs={{0,4},{4,8},{8,12},{1,5},{5,9},{9,13},{2,6},{6,10},{10,14},{3,7},{... | collective-permute-start | bytes 43784 | tf_op jit(solution)/shard_map/ppermute | solution.py:22
  181.4 1.3 collective-permute-start.11
  183.7 3.6 %collective-permute-done.11 = bf16[1,24,304]{2,0,1:T(2,128)(2,1)S(1)} collective-permute-done((bf16[1,24,304]{2,0,1:T(2,128)(2,1)S(1)}, bf16[1,24,304]{2,0,1:T(2,128)(2,1)S(1)}, u32[]{:S(2)}, u32[]{:S(2)}) %collective-permute-start.11) | collective-permute-done | bytes 14624 | tf_op jit(solution)/shard_map/ppermute | solution.py:23
  187.3 2.2 collective-permute-start.12
  189.5 1.5 collective-permute-start.13
  191.4 3.7 %collective-permute-done.13 = bf16[18,1,304]{2,0,1:T(8,128)(2,1)S(1)} collective-permute-done((bf16[18,1,304]{2,0,1:T(8,128)(2,1)S(1)}, bf16[18,1,304]{2,0,1:T(8,128)(2,1)S(1)}, u32[]{:S(2)}, u32[]{:S(2)}) %collective-permute-start.13) | collective-permute-done | bytes 10976 | tf_op jit(solution)/shard_map/ppermute | solution.py:23
  197.0 5.3 %concatenate.122 = bf16[384,2736]{1,0:T(8,128)(2,1)} concatenate(bf16[384,304]{1,0:T(8,128)(2,1)S(1)} %bitcast.100, bf16[384,304]{1,0:T(8,128)(2,1)S(1)} %bitcast.98, bf16[384,304]{1,0:T(8,128)(2,1)S(1)} %bitcast.101, bf16[384,304]{1,0:T(8,128)(2,1)S(1)} %bitcast.102, bf16[384,256]{1,0:T(8,128)(2,1)} %convert_element_type.69, bf16[384,48]{1,0:T(8,128)(2,1)} %copy-done.1, ...), dimensions={1} | concatenate | bytes 4202496 | tf_op jit(solution)/shard_map/concatenate | solution.py:51
  202.3 2.3 %fusion.10 = bf16[384,256]{1,0:T(8,128)(2,1)S(1)} fusion(bf16[384,2736]{1,0:T(8,128)(2,1)} %concatenate.122, bf16[2736,256]{1,0:T(8,128)(2,1)S(1)} %bitcast.88, f32[256]{0:T(256)S(1)} %copy-done.9), kind=kOutput, calls=%fused_computation.10 | convolution fusion | flops 538214400 | bytes 3699712 | tf_op jit(solution)/shard_map/dot_general | solution.py:53
  204.7 2.8 %collective-permute-start.14 = (bf16[1,24,256]{2,1,0:T(8,128)(2,1)S(1)}, bf16[1,24,256]{2,1,0:T(8,128)(2,1)S(1)}, u32[]{:S(2)}, u32[]{:S(2)}) collective-permute-start(bf16[1,24,256]{2,1,0:T(8,128)(2,1)S(1)} %get-tuple-element.56), channel_id=1, source_target_pairs={{0,4},{4,8},{8,12},{1,5},{5,9},{9,13},{2,6},{6,10},{10,14},{3,7},{... | collective-permute-start | bytes 36872 | tf_op jit(solution)/shard_map/ppermute | solution.py:22
  207.5 1.3 collective-permute-start.15
  208.9 4.2 %collective-permute-done.15 = bf16[1,24,256]{2,1,0:T(8,128)(2,1)S(1)} collective-permute-done((bf16[1,24,256]{2,1,0:T(8,128)(2,1)S(1)}, bf16[1,24,256]{2,1,0:T(8,128)(2,1)S(1)}, u32[]{:S(2)}, u32[]{:S(2)}) %collective-permute-start.15) | collective-permute-done | bytes 12320 | tf_op jit(solution)/shard_map/ppermute | solution.py:23
  213.1 1.9 collective-permute-start.16
  215.0 1.3 collective-permute-start.17
  216.5 4.2 %collective-permute-done.17 = bf16[18,1,256]{2,1,0:T(2,128)(2,1)S(1)} collective-permute-done((bf16[18,1,256]{2,1,0:T(2,128)(2,1)S(1)}, bf16[18,1,256]{2,1,0:T(2,128)(2,1)S(1)}, u32[]{:S(2)}, u32[]{:S(2)}) %collective-permute-start.17) | collective-permute-done | bytes 9248 | tf_op jit(solution)/shard_map/ppermute | solution.py:23
  221.2 1.1 copy-done.7
  222.3 1.3 fusion.9
  (94 shorter events, 7.9 us)
Async XLA Ops:
  6.5 195.8 %copy-start = (bf16[3,3,304,256]{3,2,1,0:T(8,128)(2,1)S(1)}, bf16[3,3,304,256]{3,2,1,0:T(8,128)(2,1)}, u32[]{:S(2)}) copy-start(bf16[3,3,304,256]{3,2,1,0:T(8,128)(2,1)} %param.24) | copy-start | bytes 4202500
  6.5 81.9 %all-gather.2.cloned.1.call-start = ((), (), s32[]{:S(2)}) async-start(), calls=%async_computation.1 | async-start | bytes 1966080 | tf_op jit(solution)/shard_map/all_gather | solution.py:126
  105.3 7.1 %collective-permute-start.4 = (f32[32,12,64]{2,1,0:T(8,128)S(1)}, f32[32,12,64]{2,1,0:T(8,128)S(1)}, u32[]{:S(2)}, u32[]{:S(2)}) collective-permute-start(f32[32,12,64]{2,1,0:T(8,128)S(1)} %get-tuple-element.21), channel_id=1, source_target_pairs={{0,3},{4,7},{8,11},{12,15},{16,19},{20,23},{24,27},{28,31}} | collective-permute-start | bytes 294920 | tf_op jit(solution)/shard_map/ppermute | solution.py:12
  106.6 11.1 %collective-permute-start.5 = (f32[32,12,64]{2,1,0:T(8,128)S(1)}, f32[32,12,64]{2,1,0:T(8,128)S(1)}, u32[]{:S(2)}, u32[]{:S(2)}) collective-permute-start(f32[32,12,64]{2,1,0:T(8,128)S(1)} %get-tuple-element.22), channel_id=1, source_target_pairs={{3,0},{7,4},{11,8},{15,12},{19,16},{23,20},{27,24},{31,28}} | collective-permute-start | bytes 294920 | tf_op jit(solution)/shard_map/ppermute | solution.py:12
  121.6 7.1 %collective-permute-start.2 = (f32[32,12,64]{2,1,0:T(8,128)S(1)}, f32[32,12,64]{2,1,0:T(8,128)S(1)}, u32[]{:S(2)}, u32[]{:S(2)}) collective-permute-start(f32[32,12,64]{2,1,0:T(8,128)S(1)} %get-tuple-element.26), channel_id=1, source_target_pairs={{0,2},{1,3},{4,6},{5,7},{8,10},{9,11},{12,14},{13,15},{16,18},{17,... | collective-permute-start | bytes 294920 | tf_op jit(solution)/shard_map/ppermute | solution.py:12
  122.9 12.9 %collective-permute-start.3 = (f32[32,12,64]{2,1,0:T(8,128)S(1)}, f32[32,12,64]{2,1,0:T(8,128)S(1)}, u32[]{:S(2)}, u32[]{:S(2)}) collective-permute-start(f32[32,12,64]{2,1,0:T(8,128)S(1)} %get-tuple-element.27), channel_id=1, source_target_pairs={{2,0},{3,1},{6,4},{7,5},{10,8},{11,9},{14,12},{15,13},{18,16},{19,... | collective-permute-start | bytes 294920 | tf_op jit(solution)/shard_map/ppermute | solution.py:12
  135.8 4.0 %copy-start.8 = (bf16[2048,64]{0,1:T(8,128)(2,1)S(1)}, bf16[2048,64]{0,1:T(8,128)(2,1)}, u32[]{:S(2)}) copy-start(bf16[2048,64]{0,1:T(8,128)(2,1)} %param.18) | copy-start | bytes 786436
  137.1 5.2 %collective-permute-start = (f32[32,12,64]{2,1,0:T(8,128)S(1)}, f32[32,12,64]{2,1,0:T(8,128)S(1)}, u32[]{:S(2)}, u32[]{:S(2)}) collective-permute-start(f32[32,12,64]{2,1,0:T(8,128)S(1)} %get-tuple-element.25), channel_id=1, source_target_pairs={{0,1},{1,2},{2,3},{4,5},{5,6},{6,7},{8,9},{9,10},{10,11},{12,13},{... | collective-permute-start | bytes 294920 | tf_op jit(solution)/shard_map/ppermute | solution.py:12
  138.5 8.3 %collective-permute-start.1 = (f32[32,12,64]{2,1,0:T(8,128)S(1)}, f32[32,12,64]{2,1,0:T(8,128)S(1)}, u32[]{:S(2)}, u32[]{:S(2)}) collective-permute-start(f32[32,12,64]{2,1,0:T(8,128)S(1)} %get-tuple-element.24), channel_id=1, source_target_pairs={{1,0},{2,1},{3,2},{5,4},{6,5},{7,6},{9,8},{10,9},{11,10},{13,12},{... | collective-permute-start | bytes 294920 | tf_op jit(solution)/shard_map/ppermute | solution.py:12
  140.1 12.4 %copy-start.2 = (bf16[1280,256]{1,0:T(8,128)(2,1)S(1)}, bf16[1280,256]{1,0:T(8,128)(2,1)}, u32[]{:S(2)}) copy-start(bf16[1280,256]{1,0:T(8,128)(2,1)} %param.20) | copy-start | bytes 1966084
  148.8 9.9 %copy-start.5 = (f32[256]{0:T(256)S(1)}, f32[256]{0:T(256)}, u32[]{:S(2)}) copy-start(f32[256]{0:T(256)} %param.21) | copy-start | bytes 3076
  148.8 9.4 %all-to-all-start = ((bf16[32,12,320]{2,1,0:T(8,128)(2,1)}), bf16[32,12,320]{2,1,0:T(8,128)(2,1)S(1)}, u32[]{:S(2)}, u32[]{:S(2)}) async-start(bf16[32,12,320]{2,1,0:T(8,128)(2,1)} %concatenate.103), calls=%async_computation | async-start | bytes 786432 | tf_op jit(solution)/shard_map/all_to_all | solution.py:166
  152.4 19.5 %copy-start.3 = (bf16[16,24,256]{2,1,0:T(8,128)(2,1)S(1)}, bf16[16,24,256]{2,1,0:T(8,128)(2,1)}, u32[]{:S(2)}) copy-start(bf16[16,24,256]{2,1,0:T(8,128)(2,1)} %param.15) | copy-start | bytes 589828
  152.5 19.5 %copy-start.4 = (bf16[256,48]{0,1:T(8,128)(2,1)S(1)}, bf16[256,48]{0,1:T(8,128)(2,1)}, u32[]{:S(2)}) copy-start(bf16[256,48]{0,1:T(8,128)(2,1)} %param.22) | copy-start | bytes 73732
  152.5 19.5 %copy-start.6 = (f32[48]{0:T(128)S(1)}, f32[48]{0:T(128)}, u32[]{:S(2)}) copy-start(f32[48]{0:T(128)} %param.23) | copy-start | bytes 580
  159.1 4.7 %collective-permute-start.6 = (bf16[1,12,256]{2,1,0:T(8,128)(2,1)S(1)}, bf16[1,12,256]{2,1,0:T(8,128)(2,1)S(1)}, u32[]{:S(2)}, u32[]{:S(2)}) collective-permute-start(bf16[1,12,256]{2,1,0:T(8,128)(2,1)S(1)} %get-tuple-element.67), channel_id=1, source_target_pairs={{0,4},{4,8},{8,12},{1,5},{5,9},{9,13},{2,6},{6,10},{10,14},{3,7},{... | collective-permute-start | bytes 18440 | tf_op jit(solution)/shard_map/ppermute | solution.py:22
  162.5 5.5 %collective-permute-start.7 = (bf16[1,12,256]{2,1,0:T(8,128)(2,1)S(1)}, bf16[1,12,256]{2,1,0:T(8,128)(2,1)S(1)}, u32[]{:S(2)}, u32[]{:S(2)}) collective-permute-start(bf16[1,12,256]{2,1,0:T(8,128)(2,1)S(1)} %get-tuple-element.66), channel_id=1, source_target_pairs={{4,0},{8,4},{12,8},{5,1},{9,5},{13,9},{6,2},{10,6},{14,10},{7,3},{... | collective-permute-start | bytes 18440 | tf_op jit(solution)/shard_map/ppermute | solution.py:23
  168.0 4.3 %collective-permute-start.8 = (bf16[10,1,256]{2,1,0:T(2,128)(2,1)S(1)}, bf16[10,1,256]{2,1,0:T(2,128)(2,1)S(1)}, u32[]{:S(2)}, u32[]{:S(2)}) collective-permute-start(bf16[10,1,256]{2,1,0:T(2,128)(2,1)S(1)} %get-tuple-element.64), channel_id=1, source_target_pairs={{0,1},{1,2},{2,3},{4,5},{5,6},{6,7},{8,9},{9,10},{10,11},{12,13},{... | collective-permute-start | bytes 15368 | tf_op jit(solution)/shard_map/ppermute | solution.py:22
  170.7 5.6 %collective-permute-start.9 = (bf16[10,1,256]{2,1,0:T(2,128)(2,1)S(1)}, bf16[10,1,256]{2,1,0:T(2,128)(2,1)S(1)}, u32[]{:S(2)}, u32[]{:S(2)}) collective-permute-start(bf16[10,1,256]{2,1,0:T(2,128)(2,1)S(1)} %get-tuple-element.65), channel_id=1, source_target_pairs={{1,0},{2,1},{3,2},{5,4},{6,5},{7,6},{9,8},{10,9},{11,10},{13,12},{... | collective-permute-start | bytes 15368 | tf_op jit(solution)/shard_map/ppermute | solution.py:23
  172.3 4.2 %copy-start.1 = (bf16[384,48]{1,0:T(8,128)(2,1)}, bf16[384,48]{1,0:T(8,128)(2,1)S(1)}, u32[]{:S(2)}) copy-start(bf16[384,48]{1,0:T(8,128)(2,1)S(1)} %copy.30) | copy-start | bytes 110596
  177.1 6.6 %collective-permute-start.10 = (bf16[1,24,304]{2,0,1:T(2,128)(2,1)S(1)}, bf16[1,24,304]{2,0,1:T(2,128)(2,1)S(1)}, u32[]{:S(2)}, u32[]{:S(2)}) collective-permute-start(bf16[1,24,304]{2,0,1:T(2,128)(2,1)S(1)} %get-tuple-element.46), channel_id=1, source_target_pairs={{0,4},{4,8},{8,12},{1,5},{5,9},{9,13},{2,6},{6,10},{10,14},{3,7},{... | collective-permute-start | bytes 43784 | tf_op jit(solution)/shard_map/ppermute | solution.py:22
  181.4 5.9 %collective-permute-start.11 = (bf16[1,24,304]{2,0,1:T(2,128)(2,1)S(1)}, bf16[1,24,304]{2,0,1:T(2,128)(2,1)S(1)}, u32[]{:S(2)}, u32[]{:S(2)}) collective-permute-start(bf16[1,24,304]{2,0,1:T(2,128)(2,1)S(1)} %get-tuple-element.47), channel_id=1, source_target_pairs={{4,0},{8,4},{12,8},{5,1},{9,5},{13,9},{6,2},{10,6},{14,10},{7,3},{... | collective-permute-start | bytes 43784 | tf_op jit(solution)/shard_map/ppermute | solution.py:23
  187.3 4.1 %collective-permute-start.12 = (bf16[18,1,304]{2,0,1:T(8,128)(2,1)S(1)}, bf16[18,1,304]{2,0,1:T(8,128)(2,1)S(1)}, u32[]{:S(2)}, u32[]{:S(2)}) collective-permute-start(bf16[18,1,304]{2,0,1:T(8,128)(2,1)S(1)} %get-tuple-element.37), channel_id=1, source_target_pairs={{0,1},{1,2},{2,3},{4,5},{5,6},{6,7},{8,9},{9,10},{10,11},{12,13},{... | collective-permute-start | bytes 32840 | tf_op jit(solution)/shard_map/ppermute | solution.py:22
  189.5 5.7 %collective-permute-start.13 = (bf16[18,1,304]{2,0,1:T(8,128)(2,1)S(1)}, bf16[18,1,304]{2,0,1:T(8,128)(2,1)S(1)}, u32[]{:S(2)}, u32[]{:S(2)}) collective-permute-start(bf16[18,1,304]{2,0,1:T(8,128)(2,1)S(1)} %get-tuple-element.36), channel_id=1, source_target_pairs={{1,0},{2,1},{3,2},{5,4},{6,5},{7,6},{9,8},{10,9},{11,10},{13,12},{... | collective-permute-start | bytes 32840 | tf_op jit(solution)/shard_map/ppermute | solution.py:23
  197.0 5.3 %copy-start.9 = (f32[256]{0:T(256)S(1)}, f32[256]{0:T(256)}, u32[]{:S(2)}) copy-start(f32[256]{0:T(256)} %param.25) | copy-start | bytes 3076
  204.7 4.2 %collective-permute-start.14 = (bf16[1,24,256]{2,1,0:T(8,128)(2,1)S(1)}, bf16[1,24,256]{2,1,0:T(8,128)(2,1)S(1)}, u32[]{:S(2)}, u32[]{:S(2)}) collective-permute-start(bf16[1,24,256]{2,1,0:T(8,128)(2,1)S(1)} %get-tuple-element.56), channel_id=1, source_target_pairs={{0,4},{4,8},{8,12},{1,5},{5,9},{9,13},{2,6},{6,10},{10,14},{3,7},{... | collective-permute-start | bytes 36872 | tf_op jit(solution)/shard_map/ppermute | solution.py:22
  207.5 5.6 %collective-permute-start.15 = (bf16[1,24,256]{2,1,0:T(8,128)(2,1)S(1)}, bf16[1,24,256]{2,1,0:T(8,128)(2,1)S(1)}, u32[]{:S(2)}, u32[]{:S(2)}) collective-permute-start(bf16[1,24,256]{2,1,0:T(8,128)(2,1)S(1)} %get-tuple-element.57), channel_id=1, source_target_pairs={{4,0},{8,4},{12,8},{5,1},{9,5},{13,9},{6,2},{10,6},{14,10},{7,3},{... | collective-permute-start | bytes 36872 | tf_op jit(solution)/shard_map/ppermute | solution.py:23
  213.1 3.4 %collective-permute-start.16 = (bf16[18,1,256]{2,1,0:T(2,128)(2,1)S(1)}, bf16[18,1,256]{2,1,0:T(2,128)(2,1)S(1)}, u32[]{:S(2)}, u32[]{:S(2)}) collective-permute-start(bf16[18,1,256]{2,1,0:T(2,128)(2,1)S(1)} %get-tuple-element.53), channel_id=1, source_target_pairs={{0,1},{1,2},{2,3},{4,5},{5,6},{6,7},{8,9},{9,10},{10,11},{12,13},{... | collective-permute-start | bytes 27656 | tf_op jit(solution)/shard_map/ppermute | solution.py:22
  215.0 5.7 %collective-permute-start.17 = (bf16[18,1,256]{2,1,0:T(2,128)(2,1)S(1)}, bf16[18,1,256]{2,1,0:T(2,128)(2,1)S(1)}, u32[]{:S(2)}, u32[]{:S(2)}) collective-permute-start(bf16[18,1,256]{2,1,0:T(2,128)(2,1)S(1)} %get-tuple-element.52), channel_id=1, source_target_pairs={{1,0},{2,1},{3,2},{5,4},{6,5},{7,6},{9,8},{10,9},{11,10},{13,12},{... | collective-permute-start | bytes 27656 | tf_op jit(solution)/shard_map/ppermute | solution.py:23
  221.0 1.3 copy-start.7
  221.0 1.3 copy-start.10
Sparse Core Ops, SparseCore 0:
  9.2 33.8 all-gather.1
where the time goes:
time: 232 us; the launch traced here: 230 us
  blocking collectives  79.2 us (34%)
  waiting for transfers between devices  58.5 us (25%)
  starting transfers between devices  36.6 us (16%)
  local copies, waits for them, and re-layouts  20.3 us (9%)
  between operations  14.1 us (6%)
  matrix products  12.5 us (5%)
  other arithmetic  9.36 us (4%)
    psum x1, blocking collectives, on_device(): scene_sum, full_bias = lax.psum((tile_sum, spread_bias), ('row', 'col'))  79.2 us
    ppermute x6, waiting for transfers between devices, from_behind(): return lax.ppermute(value, axis, pairs)  28 us
    ppermute x6, waiting for transfers between devices, padded_2(): after = lax.ppermute(first, axis, down)  23.8 us
    ppermute x6, starting transfers between devices, padded_2(): before = lax.ppermute(last, axis, up)  17.2 us
    dot_general x1, matrix products, on_device(): jnp.dot(piece.reshape(-1, in_width), stacked, preferred_element_type=jnp....  8.11 us
    ppermute x6, starting transfers between devices, padded_2(): after = lax.ppermute(first, axis, down)  7.93 us
    ppermute x6, starting transfers between devices, from_behind(): return lax.ppermute(value, axis, pairs)  7.79 us
    all_to_all x1, waiting for transfers between devices, on_device(): lax.all_to_all(branches, 'row', split_axis=0, concat_axis=2, tiled=True)  5.73 us
  transfers between devices with their start and end apart: 20, of which 15 were waited for; matrix products, arithmetic and copies ran while one was open for 2% of the time, Pallas kernels for 0%

commit v1 on v0

v1 whole, which is shorter than its diff:
```python
import functools

import jax
import jax.numpy as jnp
import numpy as np
from jax import lax
from jax.experimental import pallas as pl
from jax.experimental.pallas import tpu as pltpu
from jax.sharding import PartitionSpec as P

RATES = (12, 24, 36)
MESH = pl.DeviceIdType.MESH
F32 = jnp.float32
BF16 = jnp.bfloat16


def up16(value):
    return -(-value // 16) * 16


class Plan:
    def __init__(self, rows, cols, tile_rows, tile_cols):
        self.rows, self.cols = rows, cols
        self.tr, self.tc = tile_rows, tile_cols
        self.tile = tile_rows * tile_cols
        self.height = rows * tile_rows
        self.pixels = self.height * tile_cols
        self.half = self.pixels // 2
        self.lead = up16(2 * tile_cols)
        self.span = self.tile + 2 * self.lead
        self.cstrip = up16((tile_rows + 4) * 2)
        self.fr, self.fc = 2 * tile_rows, 2 * tile_cols
        self.wr, self.wc = self.fr + 4, self.fc + 4
        self.width = 32 * (-(-self.wc // 32))
        self.window = self.wr * self.width
        self.lhalo = 2 * self.fc
        self.low = self.wr * self.fc
        self.lstrip = up16(self.wr * 2)
        self.taps = []
        for number, rate in enumerate(RATES):
            for tap in range(3):
                if abs(tap - 1) * rate < self.height:
                    self.taps.append((number, tap))

    def upsample(self):
        own = np.zeros((9, self.window, self.span), np.float32)
        side = np.zeros((9, self.window, 2 * self.cstrip), np.float32)

        def terms(fine, length, first, last):
            if (first and fine < 0) or (last and fine >= 2 * length):
                return []
            middle = fine // 2
            other = middle - 1 if fine % 2 == 0 else middle + 1
            found = []
            for place, weight in ((middle, 0.75), (other, 0.25)):
                place = max(place, 0) if first else place
                place = min(place, length - 1) if last else place
                found.append((place, weight))
            return found

        for kind in range(9):
            top, bottom = kind // 3 == 0, kind // 3 == 2
            left, right = kind % 3 == 0, kind % 3 == 2
            for a in range(self.wr):
                for b in range(self.wc):
                    at = a * self.width + b
                    for y, wy in terms(a - 2, self.tr, top, bottom):
                        for x, wx in terms(b - 2, self.tc, left, right):
                            if x < 0:
                                side[kind, at, (y + 2) * 2 + x + 2] += wy * wx
                            elif x >= self.tc:
                                side[kind, at, self.cstrip + (y + 2) * 2 + x - self.tc] += wy * wx
                            else:
                                own[kind, at, y * self.tc + x + self.lead] += wy * wx
        return own, side

    def coarse_strips(self):
        pick = np.zeros((2 * self.cstrip, self.span), np.float32)
        for y in range(-2, self.tr + 2):
            for x in range(2):
                pick[(y + 2) * 2 + x, y * self.tc + x + self.lead] = 1
                pick[self.cstrip + (y + 2) * 2 + x, y * self.tc + self.tc - 2 + x + self.lead] = 1
        return pick

    def low_strips(self):
        pick = np.zeros((2 * self.lstrip, self.low), np.float32)
        for y in range(self.wr):
            for x in range(2):
                pick[y * 2 + x, y * self.fc + x] = 1
                pick[self.lstrip + y * 2 + x, y * self.fc + self.fc - 2 + x] = 1
        return pick

    def low_window(self):
        pick = np.zeros((self.window, self.low + 2 * self.lstrip), np.float32)
        for y in range(self.wr):
            for b in range(self.wc):
                x = b - 2
                if x < 0:
                    place = self.low + y * 2 + b
                elif x >= self.fc:
                    place = self.low + self.lstrip + y * 2 + x - self.fc
                else:
                    place = y * self.fc + x
                pick[y * self.width + b, place] = 1
        return pick


def dot(a, b):
    return jnp.dot(a, b, preferred_element_type=F32)


def kernel(
    plan,
    feat_ref, low_ref, point_ref, atrous_ref, pool_ref, aspp_bias_ref, proj_ref, proj_bias_ref,
    low_weight_ref, low_bias_ref, conv1_ref, conv1_bias_ref, conv2_ref, conv2_bias_ref,
    up_own_ref, up_side_ref, cpick_ref, lpick_ref, lwindow_ref,
    out_ref,
    gathered, staged, staged_pair, weights, low_in, proj, conv1, conv2, up_own, up_side, lwindow,
    sums, zsend, zrecv, pools, branch_pool, branches, brecv, proj_blocks,
    cstrips, crecv, low_all, lsend, reduced_window, shifted, low_part, up_window, hidden,
    local_sem, feat_send, feat_recv, z_send, z_recv, pool_send, pool_recv, bp_send, bp_recv,
    b_send, b_recv, c_send, c_recv, lr_send, lr_recv, lc_send, lc_recv,
):
    rows, cols = plan.rows, plan.cols
    tile, tc, width = plan.tile, plan.tc, plan.width
    dp, row, col = lax.axis_index("dp"), lax.axis_index("row"), lax.axis_index("col")
    depth, own = point_ref.shape
    joined = own * rows

    def row_peer(step):
        return lax.rem(row + step, rows)

    def col_peer(step):
        return lax.rem(col + step, cols)

    copies = {}
    numbered = [
        ("low", low_ref, low_in),
        ("point", point_ref, staged_pair.at[0]),
        ("pool", pool_ref, staged_pair.at[1]),
        ("feat", feat_ref, gathered.at[pl.ds(pl.multiple_of(row * tile, 16), tile)]),
        ("proj", proj_ref, proj),
        ("conv1", conv1_ref, conv1),
        ("conv2", conv2_ref, conv2),
        ("lwindow", lwindow_ref, lwindow),
    ]
    kind = jnp.where(row == 0, 0, jnp.where(row == rows - 1, 2, 1)) * 3 + jnp.where(
        col == 0, 0, jnp.where(col == cols - 1, 2, 1)
    )
    numbered.append(("up_own", up_own_ref.at[kind], up_own))
    numbered.append(("up_side", up_side_ref.at[kind], up_side))
    for place, (number, tap) in enumerate(plan.taps):
        numbered.append(("tap%d" % place, atrous_ref.at[number, tap], staged.at[place]))
    for place, (name, src, dst) in enumerate(numbered):
        copies[name] = pltpu.make_async_copy(src, dst, local_sem.at[place])
        copies[name].start()

    barrier = pltpu.get_barrier_semaphore()
    for step in range(1, rows):
        pl.semaphore_signal(barrier, inc=1, device_id=(dp, row_peer(step), col), device_id_type=MESH)
    for step in range(1, cols):
        pl.semaphore_signal(barrier, inc=1, device_id=(dp, row, col_peer(step)), device_id_type=MESH)
    pl.semaphore_wait(barrier, rows + cols - 2)

    mine = pl.ds(pl.multiple_of(row * tile, 16), tile)
    feats = []
    for step in range(1, rows):
        copy = pltpu.make_async_remote_copy(
            src_ref=feat_ref, dst_ref=gathered.at[mine],
            send_sem=feat_send.at[step - 1], recv_sem=feat_recv.at[step - 1],
            device_id=(dp, row_peer(step), col), device_id_type=MESH,
        )
        copy.start()
        feats.append(copy)

    branches[pl.ds(0, plan.lead), :] = jnp.zeros((plan.lead, 4 * own), BF16)
    branches[pl.ds(plan.lead + plan.pixels, plan.lead), :] = jnp.zeros((plan.lead, 4 * own), BF16)
    distances = [rate // tc for rate in RATES]
    for number, far in enumerate(distances):
        @pl.when(col < far)
        def _():
            zrecv[number, 0] = jnp.zeros(zrecv.shape[2:], BF16)

        @pl.when(col + far >= cols)
        def _():
            zrecv[number, 1] = jnp.zeros(zrecv.shape[2:], BF16)

    low_ends = (pl.ds(0, plan.lhalo), pl.ds(plan.low - plan.lhalo, plan.lhalo))
    low_sides = (pl.ds(plan.low, plan.lstrip), pl.ds(plan.low + plan.lstrip, plan.lstrip))
    for side, edge in ((0, row == 0), (1, row == rows - 1)):
        @pl.when(edge)
        def _():
            low_all[low_ends[side], :] = jnp.zeros((plan.lhalo, low_all.shape[1]), BF16)

    for side, edge in ((0, col == 0), (1, col == cols - 1)):
        @pl.when(edge)
        def _():
            low_all[low_sides[side], :] = jnp.zeros((plan.lstrip, low_all.shape[1]), BF16)
            crecv[side] = jnp.zeros(crecv.shape[1:], BF16)

    def pair(refs, sends, recvs, along):
        made = []
        for side in range(2):
            src, dst = refs[side]
            step = -1 if side == 0 else 1
            if along == "row":
                there = row + step >= 0 if side == 0 else row + step < rows
                target = (dp, lax.rem(row + step + rows, rows), col)
            else:
                there = col + step >= 0 if side == 0 else col + step < cols
                target = (dp, row, lax.rem(col + step + cols, cols))
            made.append((there, pltpu.make_async_remote_copy(
                src_ref=src, dst_ref=dst, send_sem=sends.at[side], recv_sem=recvs.at[1 - side],
                device_id=target, device_id_type=MESH,
            ), recvs.at[side], refs[1 - side][1]))
        return made

    def start_pair(made):
        for there, copy, _, _ in made:
            @pl.when(there)
            def _():
                copy.start()

    def wait_recv_pair(made):
        for there, copy, sem, landed in made:
            @pl.when(there)
            def _():
                pltpu.make_async_copy(landed, landed, sem).wait()

    def wait_send_pair(made):
        for there, copy, _, _ in made:
            @pl.when(there)
            def _():
                copy.wait_send()

    copies["low"].wait()
    reduced = dot(low_in[...], low_weight_ref[...]) + low_bias_ref[...]
    low_all[pl.ds(plan.lhalo, plan.fr * plan.fc), :] = jnp.maximum(reduced, 0.0).astype(BF16)
    low_rows = pair(
        (
            (low_all.at[pl.ds(plan.lhalo, plan.lhalo)], low_all.at[low_ends[1]]),
            (low_all.at[pl.ds(plan.low - 2 * plan.lhalo, plan.lhalo)], low_all.at[low_ends[0]]),
        ),
        lr_send, lr_recv, "row",
    )
    start_pair(low_rows)

    piece = min(256, depth)

    def join(place):
        number, tap = plan.taps[place]
        copies["tap%d" % place].wait()

        def body(index, carry):
            at = pl.ds(pl.multiple_of(index * piece, 16), piece)
            parts = [staged[place, j, at, :] for j in (0, 2, 1)]
            if tap == 1 and number < 2:
                parts.append(staged_pair[number, at, :])
            else:
                parts.append(jnp.zeros((piece, own), BF16))
            weights[place, at, :] = jnp.concatenate(parts, axis=1)
            return carry

        lax.fori_loop(0, depth // piece, body, 0)

    copies["point"].wait()
    copies["pool"].wait()
    for place in range(len(plan.taps)):
        join(place)

    wait_recv_pair(low_rows)
    lsend[...] = dot(lpick_ref[...], low_all[pl.ds(0, plan.low), :]).astype(BF16)
    low_cols = pair(
        (
            (lsend.at[pl.ds(0, plan.lstrip)], low_all.at[low_sides[1]]),
            (lsend.at[pl.ds(plan.lstrip, plan.lstrip)], low_all.at[low_sides[0]]),
        ),
        lc_send, lc_recv, "col",
    )
    start_pair(low_cols)

    copies["proj"].wait()
    for w in range(rows):
        for branch in range(4):
            proj_blocks[w, pl.ds(branch * own, own), :] = proj[
                pl.ds(branch * joined + w * own, own), :
            ]

    wait_recv_pair(low_cols)
    copies["lwindow"].wait()
    copies["conv1"].wait()
    reduced_window[...] = dot(lwindow[...], low_all[...]).astype(BF16)
    wide = conv1.shape[3]
    fine = wide if plan is None else conv1.shape[2] - low_all.shape[1]
    hidden_px = (plan.wr - 2) * width
    out_px = plan.fr * width
    tail = jnp.zeros((8, wide), F32)
    for j in range(2):
        shifted[j, pl.ds(hidden_px, 8), :] = tail
    for j in range(3):
        total = None
        for i in range(3):
            term = dot(
                reduced_window[pl.ds(i * width, hidden_px), :],
                conv1[i, j, pl.ds(fine, low_all.shape[1]), :],
            )
            total = term if total is None else total + term
        if j == 0:
            low_part[...] = total + conv1_bias_ref[...]
        else:
            shifted[j - 1, pl.ds(0, hidden_px), :] = total
    low_part[...] += shifted[0, pl.ds(1, hidden_px), :] + shifted[1, pl.ds(2, hidden_px), :]

    copies["feat"].wait()
    for copy in feats:
        copy.wait_recv()

    half = plan.half
    sideways = [None, None, None]
    pool_copies = []
    for number in (2, 1, 0):
        rate = RATES[number]
        for place, (which, tap) in enumerate(plan.taps):
            if which == number and tap == 1:
                sums[number] = dot(gathered[...], weights[place])
        for place, (which, tap) in enumerate(plan.taps):
            if which == number and tap != 1:
                offset = (tap - 1) * rate
                begin, end = max(0, -offset), min(plan.height, plan.height - offset)
                size = (end - begin) * tc
                sums[number, pl.ds(begin * tc, size), :] += dot(
                    gathered[pl.ds((begin + offset) * tc, size), :], weights[place]
                )
        for side in range(2):
            lanes = pl.ds(side * own, own)
            zsend[number, side] = jnp.concatenate(
                [sums[number, pl.ds(0, half), lanes], sums[number, pl.ds(half, half), lanes]], axis=1
            ).astype(BF16)
        made = []
        for side, far in ((0, distances[number]), (1, -distances[number])):
            there = col + far < cols if far > 0 else col + far >= 0
            come = col - far < cols if far < 0 else col - far >= 0
            copy = pltpu.make_async_remote_copy(
                src_ref=zsend.at[number, side], dst_ref=zrecv.at[number, side],
                send_sem=z_send.at[number, side], recv_sem=z_recv.at[number, side],
                device_id=(dp, row, lax.rem(col + far + 4 * cols, cols)), device_id_type=MESH,
            )
            made.append((there, come, copy))

            @pl.when(there)
            def _():
                copy.start()
        sideways[number] = made
        if number == 1:
            part = jnp.sum(sums[number, :, pl.ds(3 * own, own)], axis=0, keepdims=True)
            pools[col] = jnp.broadcast_to(part, (8, own))
            for step in range(1, cols):
                copy = pltpu.make_async_remote_copy(
                    src_ref=pools.at[col], dst_ref=pools.at[col],
                    send_sem=pool_send.at[step - 1], recv_sem=pool_recv.at[step - 1],
                    device_id=(dp, row, col_peer(step)), device_id_type=MESH,
                )
                copy.start()
                pool_copies.append(copy)

    for copy in pool_copies:
        copy.wait_recv()
    pooled = pools[0]
    for place in range(1, cols):
        pooled = pooled + pools[place]
    pooled = pooled / (plan.height * cols * tc)
    last = jnp.maximum(pooled + aspp_bias_ref[pl.ds(4, 1), :], 0.0)
    branch_pool[row] = jnp.concatenate([last, last], axis=0).astype(BF16)
    bp_copies = []
    for step in range(1, rows):
        copy = pltpu.make_async_remote_copy(
            src_ref=branch_pool.at[row], dst_ref=branch_pool.at[row],
            send_sem=bp_send.at[step - 1], recv_sem=bp_recv.at[step - 1],
            device_id=(dp, row_peer(step), col), device_id_type=MESH,
        )
        copy.start()
        bp_copies.append(copy)

    def bias(number):
        return aspp_bias_ref[pl.ds(number, 1), :]

    halves = []
    for part in range(2):
        at = pl.ds(part * half, half)
        halves.append([jnp.maximum(sums[0, at, pl.ds(3 * own, own)] + bias(0), 0.0).astype(BF16)])
    for number in (2, 1, 0):
        for side, (there, come, copy) in enumerate(sideways[number]):
            @pl.when(come)
            def _():
                copy.wait_recv()
    for number in range(3):
        arrived = zrecv[number, 0].astype(F32) + zrecv[number, 1].astype(F32)
        for part in range(2):
            at = pl.ds(part * half, half)
            value = sums[number, at, pl.ds(2 * own, own)] + arrived[:, part * own:(part + 1) * own]
            halves[part].append(jnp.maximum(value + bias(number + 1), 0.0).astype(BF16))
    for part in range(2):
        branches[pl.ds(plan.lead + part * half, half), :] = jnp.concatenate(halves[part], axis=1)

    b_copies = []
    for step in range(1, rows):
        start = pl.multiple_of(row_peer(step) * tile, 16)
        copy = pltpu.make_async_remote_copy(
            src_ref=branches.at[pl.ds(start, plan.span)], dst_ref=brecv.at[row],
            send_sem=b_send.at[step - 1], recv_sem=b_recv.at[step - 1],
            device_id=(dp, row_peer(step), col), device_id_type=MESH,
        )
        copy.start()
        b_copies.append(copy)
    brecv[row] = branches[pl.ds(pl.multiple_of(row * tile, 16), plan.span), :]

    for copy in bp_copies:
        copy.wait_recv()
    constant = proj_bias_ref[...]
    for w in range(rows):
        constant = constant + dot(
            branch_pool[w], proj[pl.ds(4 * joined + w * own, own), :]
        )[0:1, :]
    for copy in b_copies:
        copy.wait_recv()
    coarse = constant
    for w in range(rows):
        coarse = coarse + dot(brecv[w], proj_blocks[w])
    coarse = jnp.maximum(coarse, 0.0).astype(BF16)

    cstrips[...] = dot(cpick_ref[...], coarse).astype(BF16)
    coarse_cols = pair(
        (
            (cstrips.at[pl.ds(0, plan.cstrip)], crecv.at[1]),
            (cstrips.at[pl.ds(plan.cstrip, plan.cstrip)], crecv.at[0]),
        ),
        c_send, c_recv, "col",
    )
    start_pair(coarse_cols)
    copies["up_own"].wait()
    copies["up_side"].wait()
    copies["conv2"].wait()
    up_sums = dot(up_own[...], coarse)
    wait_recv_pair(coarse_cols)
    strips = jnp.concatenate([crecv[0], crecv[1]], axis=0)
    up_window[...] = (up_sums + dot(up_side[...], strips)).astype(BF16)

    def convolve(source, weight, depth, size):
        wide_in = jnp.concatenate(
            [source[pl.ds(i * width, size), :] for i in range(3)], axis=1
        )
        first = None
        for j in range(3):
            stacked = jnp.concatenate(
                [weight[i, j, pl.ds(0, depth), :] for i in range(3)], axis=0
            )
            total = dot(wide_in, stacked)
            if j == 0:
                first = total
            else:
                shifted[j - 1, pl.ds(0, size), :] = total
        return first + shifted[0, pl.ds(1, size), :] + shifted[1, pl.ds(2, size), :]

    result = convolve(up_window, conv1, fine, hidden_px) + low_part[...]
    result = jnp.maximum(result, 0.0).reshape(plan.wr - 2, width, wide)
    a = lax.broadcasted_iota(jnp.int32, result.shape, 0)
    b = lax.broadcasted_iota(jnp.int32, result.shape, 1)
    low_a = jnp.where(row == 0, 1, 0)
    high_a = jnp.where(row == rows - 1, plan.fr + 1, plan.fr + 2)
    low_b = jnp.where(col == 0, 1, 0)
    high_b = jnp.where(col == cols - 1, plan.fc + 1, plan.fc + 2)
    inside = (a >= low_a) & (a < high_a) & (b >= low_b) & (b < high_b)
    result = jnp.where(inside, result, 0.0)
    hidden[...] = result.reshape(hidden_px, wide).astype(BF16)

    result = convolve(hidden, conv2, conv2.shape[2], out_px) + conv2_bias_ref[...]
    result = jnp.maximum(result, 0.0).reshape(plan.fr, width, wide)
    out_ref[...] = result[:, : plan.fc, :].astype(BF16)

    for copy in feats + pool_copies + bp_copies + b_copies:
        copy.wait_send()
    for made in sideways:
        for there, come, copy in made:
            @pl.when(there)
            def _():
                copy.wait_send()
    for made in (low_rows, low_cols, coarse_cols):
        wait_send_pair(made)


def on_device(
    plan,
    features, low_level, point_weight, atrous_weight, pool_weight, aspp_bias, proj_weight, proj_bias,
    low_weight, low_bias, conv1_weight, conv1_bias, conv2_weight, conv2_bias,
):
    depth, own = point_weight.shape
    out_width = proj_weight.shape[1]
    red = low_weight.shape[1]
    rows, cols = plan.rows, plan.cols
    taps = len(plan.taps)
    wide = conv1_weight.shape[3]
    up_own, up_side = plan.upsample()
    any_spec = pl.BlockSpec(memory_space=pl.ANY)
    vmem = pl.BlockSpec(memory_space=pltpu.VMEM)
    dma = pltpu.SemaphoreType.DMA
    hidden_px = (plan.wr - 2) * plan.width
    scratch = [
        pltpu.VMEM((plan.pixels, depth), BF16),
        pltpu.VMEM((taps, 3, depth, own), BF16),
        pltpu.VMEM((2, depth, own), BF16),
        pltpu.VMEM((taps, depth, 4 * own), BF16),
        pltpu.VMEM((plan.fr * plan.fc, low_level.shape[2]), BF16),
        pltpu.VMEM(proj_weight.shape, BF16),
        pltpu.VMEM(conv1_weight.shape, BF16),
        pltpu.VMEM(conv2_weight.shape, BF16),
        pltpu.VMEM(up_own.shape[1:], BF16),
        pltpu.VMEM(up_side.shape[1:], BF16),
        pltpu.VMEM((plan.window, plan.low + 2 * plan.lstrip), BF16),
        pltpu.VMEM((3, plan.pixels, 4 * own), F32),
        pltpu.VMEM((3, 2, plan.half, 2 * own), BF16),
        pltpu.VMEM((3, 2, plan.half, 2 * own), BF16),
        pltpu.VMEM((cols, 8, own), F32),
        pltpu.VMEM((rows, 16, own), BF16),
        pltpu.VMEM((plan.pixels + 2 * plan.lead, 4 * own), BF16),
        pltpu.VMEM((rows, plan.span, 4 * own), BF16),
        pltpu.VMEM((rows, 4 * own, out_width), BF16),
        pltpu.VMEM((2 * plan.cstrip, out_width), BF16),
        pltpu.VMEM((2, plan.cstrip, out_width), BF16),
        pltpu.VMEM((plan.low + 2 * plan.lstrip, red), BF16),
        pltpu.VMEM((2 * plan.lstrip, red), BF16),
        pltpu.VMEM((plan.window, red), BF16),
        pltpu.VMEM((2, hidden_px + 8, wide), F32),
        pltpu.VMEM((hidden_px, wide), F32),
        pltpu.VMEM((plan.window, out_width), BF16),
        pltpu.VMEM((hidden_px, wide), BF16),
        dma((10 + taps,)),
        dma((rows - 1,)), dma((rows - 1,)),
        dma((3, 2)), dma((3, 2)),
        dma((cols - 1,)), dma((cols - 1,)),
        dma((rows - 1,)), dma((rows - 1,)),
        dma((rows - 1,)), dma((rows - 1,)),
        dma((2,)), dma((2,)), dma((2,)), dma((2,)), dma((2,)), dma((2,)),
    ]
    return pl.pallas_call(
        functools.partial(kernel, plan),
        out_shape=jax.ShapeDtypeStruct((plan.fr, plan.fc, wide), BF16),
        in_specs=[
            any_spec, any_spec, any_spec, any_spec, any_spec, vmem, any_spec, vmem,
            vmem, vmem, any_spec, vmem, any_spec, vmem,
            any_spec, any_spec, vmem, vmem, any_spec,
        ],
        out_specs=vmem,
        scratch_shapes=scratch,
        compiler_params=pltpu.CompilerParams(
            collective_id=0, has_side_effects=True, vmem_limit_bytes=60 * 1024 * 1024
        ),
    )(
        features.reshape(plan.tile, depth),
        low_level.reshape(plan.fr * plan.fc, low_level.shape[2]),
        point_weight, atrous_weight, pool_weight, aspp_bias, proj_weight, proj_bias[None],
        low_weight, low_bias[None], conv1_weight, conv1_bias[None], conv2_weight, conv2_bias[None],
        jnp.asarray(up_own, BF16), jnp.asarray(up_side, BF16),
        jnp.asarray(plan.coarse_strips(), BF16), jnp.asarray(plan.low_strips(), BF16),
        jnp.asarray(plan.low_window(), BF16),
    )


def solution(mesh):
    placed = (
        P(("dp", "row"), "col", None),
        P(("dp", "row"), "col", None),
        P(None, "row"),
        P(None, None, None, None, "row"),
        P(None, "row"),
        P(None, "row"),
        P(),
        P(),
        P(),
        P(),
        P(),
        P(),
        P(),
        P(),
    )

    def local(features, *others):
        plan = Plan(mesh.shape["row"], mesh.shape["col"], features.shape[0], features.shape[1])
        return on_device(plan, features, *others)

    return jax.shard_map(
        local,
        mesh=mesh,
        in_specs=placed,
        out_specs=P(("dp", "row"), "col", None),
        check_vma=False,
    )
```

time: 232 us -> 73.3 us (0.32)
  blocking collectives: 79.2 us -> 0 us
  waiting for transfers between devices: 58.5 us -> 0 us
  Pallas kernels: 0 us -> 49 us
  starting transfers between devices: 36.6 us -> 0 us
  between operations: 14.1 us -> 0.02 us
  matrix products: 12.5 us -> 0 us
  other arithmetic: 9.36 us -> 0 us
  local copies, waits for them, and re-layouts: 20.3 us -> 23.7 us
    psum x1 -> x0, blocking collectives: 79.2 us -> none  [on_device(): scene_sum, full_bias = lax.psum((tile_sum, spread_bias), ('row', 'col'))]
    ppermute x18 -> x0, waiting for transfers between devices: 52 us -> none  [the longest x6 28 us: from_behind(): return lax.ppermute(value, axis, pairs)]
    pallas_call x0 -> x1, Pallas kernels: none -> 49 us  [on_device(): pl.pallas_call(functools.partial(kernel, plan), out_shape=jax.ShapeDtypeS...]
    ppermute x18 -> x0, starting transfers between devices: 33 us -> none  [the longest x6 17.2 us: padded_2(): before = lax.ppermute(last, axis, up)]
    unnamed x32 -> x6, local copies, waits for them, and re-layouts: 1.24 us -> 22.8 us
    dot_general x6 -> x0, matrix products: 12.5 us -> none  [the longest x1 8.11 us: on_device(): jnp.dot(piece.reshape(-1, in_width), stacked, preferred_element_type=jnp....]
    concatenate x4 -> x0, local copies, waits for them, and re-layouts: 6.27 us -> none  [the longest x2 5.28 us: convolve(): columns = jnp.concatenate(windows, axis=2)]
    all_to_all x1 -> x0, waiting for transfers between devices: 5.73 us -> none  [on_device(): lax.all_to_all(branches, 'row', split_axis=0, concat_axis=2, tiled=True)]
  transfers between devices with their start and end apart: 20 -> 0, of which waited for: 15 -> 0; matrix products, arithmetic and copies ran while one was open for 2% -> 0% of each run, Pallas kernels for 0% -> 0%
where the time goes in v1:
time: 73.3 us; the launch traced here: 72.6 us
  Pallas kernels  49 us (67%)
  local copies, waits for them, and re-layouts  23.7 us (32%)
    pallas_call x1, Pallas kernels, on_device(): pl.pallas_call(functools.partial(kernel, plan), out_shape=jax.ShapeDtypeS...  49 us
    unnamed x6, local copies, waits for them, and re-layouts  22.8 us

profile of v1, /device:TPU:0, one launch (start us, length us, event | category | flops | bytes accessed | tf_op | source)
XLA Modules:
  0.0 72.6 jit_solution(13587608294595829860)
XLA Ops:
  0.0 1.5 %copy.29.low_weight_ref = bf16[256,48]{1,0:T(8,128)(2,1)} copy(bf16[256,48]{0,1:T(8,128)(2,1)} %param.27) | data formatting | bytes 49152 | tf_op args[8]
  1.5 1.2 %copy.25 = bf16[8,12,2048]{2,1,0:T(8,128)(2,1)S(1)} copy(bf16[8,12,2048]{2,0,1:T(8,128)(2,1)} %param.19) | data formatting | bytes 786432 | tf_op args[0]
  2.7 0.8 %reshape.6.feat_ref = bf16[96,2048]{1,0:T(8,128)(2,1)} reshape(bf16[8,12,2048]{2,1,0:T(8,128)(2,1)S(1)} %copy.25) | data formatting | bytes 786432 | tf_op jit(solution)/shard_map/reshape | solution.py:558
  3.5 2.0 %copy.26.point_ref = bf16[2048,64]{1,0:T(8,128)(2,1)} copy(bf16[2048,64]{0,1:T(8,128)(2,1)} %param.21) | data formatting | bytes 524288 | tf_op args[2]
  5.5 2.0 %copy.28.pool_ref = bf16[2048,64]{1,0:T(8,128)(2,1)} copy(bf16[2048,64]{0,1:T(8,128)(2,1)} %param.23) | data formatting | bytes 524288 | tf_op args[4]
  7.5 14.6 %copy.27.atrous_ref = bf16[3,3,3,2048,64]{4,3,2,1,0:T(8,128)(2,1)} copy(bf16[3,3,3,2048,64]{3,4,2,1,0:T(8,128)(2,1)} %param.22) | data formatting | bytes 14155776 | tf_op args[3]
  22.0 49.0 %shard_map.181 = bf16[16,24,256]{2,1,0:T(8,128)(2,1)} custom-call(bf16[96,2048]{1,0:T(8,128)(2,1)} %reshape.6.feat_ref, bf16[384,256]{1,0:T(8,128)(2,1)} %bitcast.5, bf16[2048,64]{1,0:T(8,128)(2,1)} %copy.26.point_ref, bf16[3,3,3,2048,64]{4,3,2,1,0:T(8,128)(2,1)} %copy.27.atrous_ref, bf16[2048,64]{1,0:T(8,128)(2,1)} %copy.28.pool_ref, ...), custom_call_target="tpu_custom_call" | custom-call | tf_op jit(solution)/shard_map/pallas_call | solution.py:544
  71.0 1.6 %copy.31 = bf16[16,24,256]{2,1,0:T(8,128)(2,1)} copy(bf16[16,24,256]{2,1,0:T(8,128)(2,1)} %shard_map.181) | data formatting | bytes 393216

commit v2 on v1

--- a/solution.py
+++ b/solution.py
@@ -16,6 +16,11 @@
 
 def up16(value):
     return -(-value // 16) * 16
+
+
+def table(values):
+    lanes = -values.shape[-1] % 128
+    return np.pad(values, [(0, 0)] * (values.ndim - 1) + [(0, lanes)])
 
 
 class Plan:
@@ -71,16 +76,31 @@
                             elif x >= self.tc:
                                 side[kind, at, self.cstrip + (y + 2) * 2 + x - self.tc] += wy * wx
                             else:
-                                own[kind, at, y * self.tc + x + self.lead] += wy * wx
-        return own, side
+                                own[kind, at, self.pixel(y, x)] += wy * wx
+        return table(own), table(side)
+
+    def pixel(self, y, x):
+        if y < 0:
+            return x * 2 + y + 2
+        if y >= self.tr:
+            return self.lead + self.tile + x * 2 + y - self.tr
+        return self.lead + x * self.tr + y
+
+    def row_strips(self):
+        pick = np.zeros((2 * self.lead, self.tile), np.float32)
+        for x in range(self.tc):
+            for y in range(2):
+                pick[x * 2 + y, x * self.tr + self.tr - 2 + y] = 1
+                pick[self.lead + x * 2 + y, x * self.tr + y] = 1
+        return table(pick)
 
     def coarse_strips(self):
         pick = np.zeros((2 * self.cstrip, self.span), np.float32)
         for y in range(-2, self.tr + 2):
             for x in range(2):
-                pick[(y + 2) * 2 + x, y * self.tc + x + self.lead] = 1
-                pick[self.cstrip + (y + 2) * 2 + x, y * self.tc + self.tc - 2 + x + self.lead] = 1
-        return pick
+                pick[(y + 2) * 2 + x, self.pixel(y, x)] = 1
+                pick[self.cstrip + (y + 2) * 2 + x, self.pixel(y, self.tc - 2 + x)] = 1
+        return table(pick)
 
     def low_strips(self):
         pick = np.zeros((2 * self.lstrip, self.low), np.float32)
@@ -88,7 +108,7 @@
             for x in range(2):
                 pick[y * 2 + x, y * self.fc + x] = 1
                 pick[self.lstrip + y * 2 + x, y * self.fc + self.fc - 2 + x] = 1
-        return pick
+        return table(pick)
 
     def low_window(self):
         pick = np.zeros((self.window, self.low + 2 * self.lstrip), np.float32)
@@ -102,20 +122,24 @@
                 else:
                     place = y * self.fc + x
                 pick[y * self.width + b, place] = 1
-        return pick
+        return table(pick)
 
 
 def dot(a, b):
     return jnp.dot(a, b, preferred_element_type=F32)
+
+
+def dot_t(a, b):
+    return lax.dot_general(a, b, (((1,), (1,)), ((), ())), preferred_element_type=F32)
 
 
 def kernel(
     plan,
     feat_ref, low_ref, point_ref, atrous_ref, pool_ref, aspp_bias_ref, proj_ref, proj_bias_ref,
     low_weight_ref, low_bias_ref, conv1_ref, conv1_bias_ref, conv2_ref, conv2_bias_ref,
-    up_own_ref, up_side_ref, cpick_ref, lpick_ref, lwindow_ref,
+    up_own_ref, up_side_ref, rpick_ref, cpick_ref, lpick_ref, lwindow_ref,
     out_ref,
-    gathered, staged, staged_pair, weights, low_in, proj, conv1, conv2, up_own, up_side, lwindow,
+    gathered, weights, low_in, proj, conv1, conv2, up_own, up_side, lwindow,
     sums, zsend, zrecv, pools, branch_pool, branches, brecv, proj_blocks,
     cstrips, crecv, low_all, lsend, reduced_window, shifted, low_part, up_window, hidden,
     local_sem, feat_send, feat_recv, z_send, z_recv, pool_send, pool_recv, bp_send, bp_recv,
@@ -124,7 +148,7 @@
     rows, cols = plan.rows, plan.cols
     tile, tc, width = plan.tile, plan.tc, plan.width
     dp, row, col = lax.axis_index("dp"), lax.axis_index("row"), lax.axis_index("col")
-    depth, own = point_ref.shape
+    own, depth = point_ref.shape
     joined = own * rows
 
     def row_peer(step):
@@ -136,8 +160,6 @@
     copies = {}
     numbered = [
         ("low", low_ref, low_in),
-        ("point", point_ref, staged_pair.at[0]),
-        ("pool", pool_ref, staged_pair.at[1]),
         ("feat", feat_ref, gathered.at[pl.ds(pl.multiple_of(row * tile, 16), tile)]),
         ("proj", proj_ref, proj),
         ("conv1", conv1_ref, conv1),
@@ -150,7 +172,17 @@
     numbered.append(("up_own", up_own_ref.at[kind], up_own))
     numbered.append(("up_side", up_side_ref.at[kind], up_side))
     for place, (number, tap) in enumerate(plan.taps):
-        numbered.append(("tap%d" % place, atrous_ref.at[number, tap], staged.at[place]))
+        for slot, j in enumerate((0, 2, 1)):
+            numbered.append((
+                ("tap", place, slot), atrous_ref.at[number, tap, j],
+                weights.at[place, pl.ds(slot * own, own)],
+            ))
+        if tap == 1 and number < 2:
+            numbered.append((
+                ("tap", place, 3), (point_ref, pool_ref)[number], weights.at[place, pl.ds(3 * own, own)]
+            ))
+        else:
+            weights[place, pl.ds(3 * own, own), :] = jnp.zeros((own, depth), BF16)
     for place, (name, src, dst) in enumerate(numbered):
         copies[name] = pltpu.make_async_copy(src, dst, local_sem.at[place])
         copies[name].start()
@@ -162,19 +194,43 @@
         pl.semaphore_signal(barrier, inc=1, device_id=(dp, row, col_peer(step)), device_id_type=MESH)
     pl.semaphore_wait(barrier, rows + cols - 2)
 
-    mine = pl.ds(pl.multiple_of(row * tile, 16), tile)
-    feats = []
-    for step in range(1, rows):
+    def block(owner, part=0, parts=1):
+        size = tile // parts
+        return pl.ds(pl.multiple_of(owner * tile + part * size, 16), size)
+
+    def send_block(src, owner, part, parts, target, at):
         copy = pltpu.make_async_remote_copy(
-            src_ref=feat_ref, dst_ref=gathered.at[mine],
-            send_sem=feat_send.at[step - 1], recv_sem=feat_recv.at[step - 1],
-            device_id=(dp, row_peer(step), col), device_id_type=MESH,
+            src_ref=src, dst_ref=gathered.at[block(owner, part, parts)],
+            send_sem=feat_send.at[at], recv_sem=feat_recv.at[at],
+            device_id=(dp, target, col), device_id_type=MESH,
         )
         copy.start()
-        feats.append(copy)
-
-    branches[pl.ds(0, plan.lead), :] = jnp.zeros((plan.lead, 4 * own), BF16)
-    branches[pl.ds(plan.lead + plan.pixels, plan.lead), :] = jnp.zeros((plan.lead, 4 * own), BF16)
+        return copy
+
+    feats = []
+    passing = rows == 4
+    if passing:
+        beside = row + 1 - 2 * lax.rem(row, 2)
+        across = row + 2 - 4 * (row // 2)
+        size = tile // 2
+        ends = [feat_ref.at[pl.ds(part * size, size)] for part in range(2)]
+        feats.append(send_block(ends[0], row, 0, 2, beside, 0))
+        feats.append(send_block(ends[1], row, 1, 2, across, 2))
+        feats.append(send_block(ends[1], row, 1, 2, beside, 1))
+        feats.append(send_block(ends[0], row, 0, 2, across, 3))
+    else:
+        for step in range(1, rows):
+            feats.append(send_block(feat_ref, row, 0, 1, row_peer(step), step - 1))
+
+    def pass_on():
+        if passing:
+            feats[0].wait_recv()
+            feats.append(send_block(gathered.at[block(beside, 0, 2)], beside, 0, 2, across, 4))
+            feats[1].wait_recv()
+            feats.append(send_block(gathered.at[block(across, 1, 2)], across, 1, 2, beside, 5))
+
+    branches[0, pl.ds(0, plan.lead), :] = jnp.zeros((plan.lead, 4 * own), BF16)
+    branches[rows - 1, pl.ds(plan.lead + tile, plan.lead), :] = jnp.zeros((plan.lead, 4 * own), BF16)
     distances = [rate // tc for rate in RATES]
     for number, far in enumerate(distances):
         @pl.when(col < far)
@@ -234,7 +290,7 @@
                 copy.wait_send()
 
     copies["low"].wait()
-    reduced = dot(low_in[...], low_weight_ref[...]) + low_bias_ref[...]
+    reduced = dot_t(low_in[...], low_weight_ref[...]) + low_bias_ref[...]
     low_all[pl.ds(plan.lhalo, plan.fr * plan.fc), :] = jnp.maximum(reduced, 0.0).astype(BF16)
     low_rows = pair(
         (
@@ -245,31 +301,9 @@
     )
     start_pair(low_rows)
 
-    piece = min(256, depth)
-
-    def join(place):
-        number, tap = plan.taps[place]
-        copies["tap%d" % place].wait()
-
-        def body(index, carry):
-            at = pl.ds(pl.multiple_of(index * piece, 16), piece)
-            parts = [staged[place, j, at, :] for j in (0, 2, 1)]
-            if tap == 1 and number < 2:
-                parts.append(staged_pair[number, at, :])
-            else:
-                parts.append(jnp.zeros((piece, own), BF16))
-            weights[place, at, :] = jnp.concatenate(parts, axis=1)
-            return carry
-
-        lax.fori_loop(0, depth // piece, body, 0)
-
-    copies["point"].wait()
-    copies["pool"].wait()
-    for place in range(len(plan.taps)):
-        join(place)
-
+    pass_on()
     wait_recv_pair(low_rows)
-    lsend[...] = dot(lpick_ref[...], low_all[pl.ds(0, plan.low), :]).astype(BF16)
+    lsend[...] = dot(lpick_ref[:, pl.ds(0, plan.low)], low_all[pl.ds(0, plan.low), :]).astype(BF16)
     low_cols = pair(
         (
             (lsend.at[pl.ds(0, plan.lstrip)], low_all.at[low_sides[1]]),
@@ -289,9 +323,9 @@
     wait_recv_pair(low_cols)
     copies["lwindow"].wait()
     copies["conv1"].wait()
-    reduced_window[...] = dot(lwindow[...], low_all[...]).astype(BF16)
+    reduced_window[...] = dot(lwindow[:, pl.ds(0, low_all.shape[0])], low_all[...]).astype(BF16)
     wide = conv1.shape[3]
-    fine = wide if plan is None else conv1.shape[2] - low_all.shape[1]
+    fine = conv1.shape[2] - low_all.shape[1]
     hidden_px = (plan.wr - 2) * width
     out_px = plan.fr * width
     tail = jnp.zeros((8, wide), F32)
@@ -312,7 +346,10 @@
     low_part[...] += shifted[0, pl.ds(1, hidden_px), :] + shifted[1, pl.ds(2, hidden_px), :]
 
     copies["feat"].wait()
-    for copy in feats:
+    for name, copy in copies.items():
+        if name[0] == "tap":
+            copy.wait()
+    for copy in feats[2 if passing else 0:]:
         copy.wait_recv()
 
     half = plan.half
@@ -322,15 +359,30 @@
         rate = RATES[number]
         for place, (which, tap) in enumerate(plan.taps):
             if which == number and tap == 1:
-                sums[number] = dot(gathered[...], weights[place])
+                sums[number] = dot_t(gathered[...], weights[place])
         for place, (which, tap) in enumerate(plan.taps):
             if which == number and tap != 1:
                 offset = (tap - 1) * rate
-                begin, end = max(0, -offset), min(plan.height, plan.height - offset)
-                size = (end - begin) * tc
-                sums[number, pl.ds(begin * tc, size), :] += dot(
-                    gathered[pl.ds((begin + offset) * tc, size), :], weights[place]
-                )
+                whole, rest = offset // plan.tr, offset % plan.tr
+                used = [whole, whole + 1] if rest else [whole]
+                first = max(0, used[0])
+                final = min(rows, rows + used[-1])
+                size = (final - first) * tile
+                term = dot_t(gathered[pl.ds(first * tile, size), :], weights[place])
+                if rest:
+                    term = term.reshape(size // plan.tr, plan.tr, 4 * own)
+                    term = pltpu.roll(term, plan.tr - rest, 1)
+                    upper = lax.broadcasted_iota(jnp.int32, term.shape, 1) < plan.tr - rest
+                    terms = [jnp.where(upper, term, 0.0), jnp.where(upper, 0.0, term)]
+                    terms = [value.reshape(size, 4 * own) for value in terms]
+                else:
+                    terms = [term]
+                for step, value in zip(used, terms):
+                    begin, end = max(0, -step), min(rows, rows - step)
+                    count = (end - begin) * tile
+                    if count > 0:
+                        skip = (begin + step - first) * tile
+                        sums[number, pl.ds(begin * tile, count), :] += value[skip:skip + count]
         for side in range(2):
             lanes = pl.ds(side * own, own)
             zsend[number, side] = jnp.concatenate(
@@ -399,20 +451,27 @@
             at = pl.ds(part * half, half)
             value = sums[number, at, pl.ds(2 * own, own)] + arrived[:, part * own:(part + 1) * own]
             halves[part].append(jnp.maximum(value + bias(number + 1), 0.0).astype(BF16))
-    for part in range(2):
-        branches[pl.ds(plan.lead + part * half, half), :] = jnp.concatenate(halves[part], axis=1)
+    joint = [jnp.concatenate(halves[part], axis=1) for part in range(2)]
+    joint = jnp.concatenate(joint, axis=0)
+    for place in range(rows):
+        value = joint[place * tile:(place + 1) * tile]
+        branches[place, pl.ds(plan.lead, tile), :] = value
+        ends = dot(rpick_ref[:, pl.ds(0, tile)], value).astype(BF16)
+        if place + 1 < rows:
+            branches[place + 1, pl.ds(0, plan.lead), :] = ends[: plan.lead]
+        if place > 0:
+            branches[place - 1, pl.ds(plan.lead + tile, plan.lead), :] = ends[plan.lead:]
 
     b_copies = []
     for step in range(1, rows):
-        start = pl.multiple_of(row_peer(step) * tile, 16)
         copy = pltpu.make_async_remote_copy(
-            src_ref=branches.at[pl.ds(start, plan.span)], dst_ref=brecv.at[row],
+            src_ref=branches.at[row_peer(step)], dst_ref=brecv.at[row],
             send_sem=b_send.at[step - 1], recv_sem=b_recv.at[step - 1],
             device_id=(dp, row_peer(step), col), device_id_type=MESH,
         )
         copy.start()
         b_copies.append(copy)
-    brecv[row] = branches[pl.ds(pl.multiple_of(row * tile, 16), plan.span), :]
+    brecv[row] = branches[row]
 
     for copy in bp_copies:
         copy.wait_recv()
@@ -428,7 +487,7 @@
         coarse = coarse + dot(brecv[w], proj_blocks[w])
     coarse = jnp.maximum(coarse, 0.0).astype(BF16)
 
-    cstrips[...] = dot(cpick_ref[...], coarse).astype(BF16)
+    cstrips[...] = dot(cpick_ref[:, pl.ds(0, plan.span)], coarse).astype(BF16)
     coarse_cols = pair(
         (
             (cstrips.at[pl.ds(0, plan.cstrip)], crecv.at[1]),
@@ -440,10 +499,10 @@
     copies["up_own"].wait()
     copies["up_side"].wait()
     copies["conv2"].wait()
-    up_sums = dot(up_own[...], coarse)
+    up_sums = dot(up_own[:, pl.ds(0, plan.span)], coarse)
     wait_recv_pair(coarse_cols)
     strips = jnp.concatenate([crecv[0], crecv[1]], axis=0)
-    up_window[...] = (up_sums + dot(up_side[...], strips)).astype(BF16)
+    up_window[...] = (up_sums + dot(up_side[:, pl.ds(0, 2 * plan.cstrip)], strips)).astype(BF16)
 
     def convolve(source, weight, depth, size):
         wide_in = jnp.concatenate(
@@ -493,7 +552,7 @@
     features, low_level, point_weight, atrous_weight, pool_weight, aspp_bias, proj_weight, proj_bias,
     low_weight, low_bias, conv1_weight, conv1_bias, conv2_weight, conv2_bias,
 ):
-    depth, own = point_weight.shape
+    own, depth = point_weight.shape[::-1]
     out_width = proj_weight.shape[1]
     red = low_weight.shape[1]
     rows, cols = plan.rows, plan.cols
@@ -504,24 +563,23 @@
     vmem = pl.BlockSpec(memory_space=pltpu.VMEM)
     dma = pltpu.SemaphoreType.DMA
     hidden_px = (plan.wr - 2) * plan.width
+    feat_sends = 6 if rows == 4 else rows - 1
     scratch = [
         pltpu.VMEM((plan.pixels, depth), BF16),
-        pltpu.VMEM((taps, 3, depth, own), BF16),
-        pltpu.VMEM((2, depth, own), BF16),
-        pltpu.VMEM((taps, depth, 4 * own), BF16),
+        pltpu.VMEM((taps, 4 * own, depth), BF16),
         pltpu.VMEM((plan.fr * plan.fc, low_level.shape[2]), BF16),
         pltpu.VMEM(proj_weight.shape, BF16),
         pltpu.VMEM(conv1_weight.shape, BF16),
         pltpu.VMEM(conv2_weight.shape, BF16),
         pltpu.VMEM(up_own.shape[1:], BF16),
         pltpu.VMEM(up_side.shape[1:], BF16),
-        pltpu.VMEM((plan.window, plan.low + 2 * plan.lstrip), BF16),
+        pltpu.VMEM(plan.low_window().shape, BF16),
         pltpu.VMEM((3, plan.pixels, 4 * own), F32),
         pltpu.VMEM((3, 2, plan.half, 2 * own), BF16),
         pltpu.VMEM((3, 2, plan.half, 2 * own), BF16),
         pltpu.VMEM((cols, 8, own), F32),
         pltpu.VMEM((rows, 16, own), BF16),
-        pltpu.VMEM((plan.pixels + 2 * plan.lead, 4 * own), BF16),
+        pltpu.VMEM((rows, plan.span, 4 * own), BF16),
         pltpu.VMEM((rows, plan.span, 4 * own), BF16),
         pltpu.VMEM((rows, 4 * own, out_width), BF16),
         pltpu.VMEM((2 * plan.cstrip, out_width), BF16),
@@ -533,8 +591,8 @@
         pltpu.VMEM((hidden_px, wide), F32),
         pltpu.VMEM((plan.window, out_width), BF16),
         pltpu.VMEM((hidden_px, wide), BF16),
-        dma((10 + taps,)),
-        dma((rows - 1,)), dma((rows - 1,)),
+        dma((8 + 4 * taps,)),
+        dma((feat_sends,)), dma((feat_sends,)),
         dma((3, 2)), dma((3, 2)),
         dma((cols - 1,)), dma((cols - 1,)),
         dma((rows - 1,)), dma((rows - 1,)),
@@ -547,7 +605,7 @@
         in_specs=[
             any_spec, any_spec, any_spec, any_spec, any_spec, vmem, any_spec, vmem,
             vmem, vmem, any_spec, vmem, any_spec, vmem,
-            any_spec, any_spec, vmem, vmem, any_spec,
+            any_spec, any_spec, vmem, vmem, vmem, any_spec,
         ],
         out_specs=vmem,
         scratch_shapes=scratch,
@@ -555,12 +613,12 @@
             collective_id=0, has_side_effects=True, vmem_limit_bytes=60 * 1024 * 1024
         ),
     )(
-        features.reshape(plan.tile, depth),
+        jnp.transpose(features, (1, 0, 2)).reshape(plan.tile, depth),
         low_level.reshape(plan.fr * plan.fc, low_level.shape[2]),
-        point_weight, atrous_weight, pool_weight, aspp_bias, proj_weight, proj_bias[None],
-        low_weight, low_bias[None], conv1_weight, conv1_bias[None], conv2_weight, conv2_bias[None],
+        point_weight.T, jnp.swapaxes(atrous_weight, 3, 4), pool_weight.T, aspp_bias, proj_weight,
+        proj_bias[None], low_weight.T, low_bias[None], conv1_weight, conv1_bias[None], conv2_weight, conv2_bias[None],
         jnp.asarray(up_own, BF16), jnp.asarray(up_side, BF16),
-        jnp.asarray(plan.coarse_strips(), BF16), jnp.asarray(plan.low_strips(), BF16),
+        jnp.asarray(plan.row_strips(), BF16), jnp.asarray(plan.coarse_strips(), BF16), jnp.asarray(plan.low_strips(), BF16),
         jnp.asarray(plan.low_window(), BF16),
     )
 

time: 73.3 us -> 44.1 us (0.60)
  local copies, waits for them, and re-layouts: 23.7 us -> 1.62 us
  Pallas kernels: 49 us -> 42.4 us
    unnamed x6 -> x1, local copies, waits for them, and re-layouts: 22.8 us -> 1.62 us
    pallas_call x1, Pallas kernels: 49 us -> 42.4 us  [on_device(): pl.pallas_call(functools.partial(kernel, plan), out_shape=jax.ShapeDtypeS...]
    reshape x1 -> x0, local copies, waits for them, and re-layouts: 0.84 us -> none  [on_device(): features.reshape(plan.tile, depth)]
where the time goes in v2:
time: 44.1 us; the launch traced here: 44 us
  Pallas kernels  42.4 us (96%)
  local copies, waits for them, and re-layouts  1.62 us (4%)
    pallas_call x1, Pallas kernels, on_device(): pl.pallas_call(functools.partial(kernel, plan), out_shape=jax.ShapeDtypeS...  42.4 us
    unnamed x1, local copies, waits for them, and re-layouts  1.62 us

profile of v2, /device:TPU:0, one launch (start us, length us, event | category | flops | bytes accessed | tf_op | source)
XLA Modules:
  0.0 44.0 jit_solution(4733291706221082281)
XLA Ops:
  0.0 42.4 %shard_map.190 = bf16[16,24,256]{2,1,0:T(8,128)(2,1)} custom-call(bf16[96,2048]{1,0:T(8,128)(2,1)} %bitcast.13, bf16[384,256]{1,0:T(8,128)(2,1)} %bitcast.16, bf16[64,2048]{1,0:T(8,128)(2,1)} %bitcast.14, bf16[3,3,3,64,2048]{4,3,2,1,0:T(8,128)(2,1)} %bitcast.12, bf16[64,2048]{1,0:T(8,128)(2,1)} %bitcast.15, f32[5,64]{1,0:T(8,128)} %aspp_bias_ref.1, ...), custom_call_target="tpu_custom_call" | custom-call | tf_op jit(solution)/shard_map/pallas_call | solution.py:602
  42.4 1.6 %copy.22 = bf16[16,24,256]{2,1,0:T(8,128)(2,1)} copy(bf16[16,24,256]{2,1,0:T(8,128)(2,1)} %shard_map.190) | data formatting | bytes 393216

commit v3 on v2

--- a/solution.py
+++ b/solution.py
@@ -156,6 +156,41 @@
 
     def col_peer(step):
         return lax.rem(col + step, cols)
+
+    barrier = pltpu.get_barrier_semaphore()
+    for step in range(1, rows):
+        pl.semaphore_signal(barrier, inc=1, device_id=(dp, row_peer(step), col), device_id_type=MESH)
+    for step in range(1, cols):
+        pl.semaphore_signal(barrier, inc=1, device_id=(dp, row, col_peer(step)), device_id_type=MESH)
+    pl.semaphore_wait(barrier, rows + cols - 2)
+
+    def block(owner, part=0, parts=1):
+        size = tile // parts
+        return pl.ds(pl.multiple_of(owner * tile + part * size, 16), size)
+
+    def send_block(src, owner, part, parts, target, at):
+        copy = pltpu.make_async_remote_copy(
+            src_ref=src, dst_ref=gathered.at[block(owner, part, parts)],
+            send_sem=feat_send.at[at], recv_sem=feat_recv.at[at],
+            device_id=(dp, target, col), device_id_type=MESH,
+        )
+        copy.start()
+        return copy
+
+    feats = []
+    passing = rows == 4
+    if passing:
+        beside = row + 1 - 2 * lax.rem(row, 2)
+        across = row + 2 - 4 * (row // 2)
+        size = tile // 2
+        ends = [feat_ref.at[pl.ds(part * size, size)] for part in range(2)]
+        feats.append(send_block(ends[0], row, 0, 2, beside, 0))
+        feats.append(send_block(ends[1], row, 1, 2, across, 2))
+        feats.append(send_block(ends[1], row, 1, 2, beside, 1))
+        feats.append(send_block(ends[0], row, 0, 2, across, 3))
+    else:
+        for step in range(1, rows):
+            feats.append(send_block(feat_ref, row, 0, 1, row_peer(step), step - 1))
 
     copies = {}
     numbered = [
@@ -187,41 +222,6 @@
         copies[name] = pltpu.make_async_copy(src, dst, local_sem.at[place])
         copies[name].start()
 
-    barrier = pltpu.get_barrier_semaphore()
-    for step in range(1, rows):
-        pl.semaphore_signal(barrier, inc=1, device_id=(dp, row_peer(step), col), device_id_type=MESH)
-    for step in range(1, cols):
-        pl.semaphore_signal(barrier, inc=1, device_id=(dp, row, col_peer(step)), device_id_type=MESH)
-    pl.semaphore_wait(barrier, rows + cols - 2)
-
-    def block(owner, part=0, parts=1):
-        size = tile // parts
-        return pl.ds(pl.multiple_of(owner * tile + part * size, 16), size)
-
-    def send_block(src, owner, part, parts, target, at):
-        copy = pltpu.make_async_remote_copy(
-            src_ref=src, dst_ref=gathered.at[block(owner, part, parts)],
-            send_sem=feat_send.at[at], recv_sem=feat_recv.at[at],
-            device_id=(dp, target, col), device_id_type=MESH,
-        )
-        copy.start()
-        return copy
-
-    feats = []
-    passing = rows == 4
-    if passing:
-        beside = row + 1 - 2 * lax.rem(row, 2)
-        across = row + 2 - 4 * (row // 2)
-        size = tile // 2
-        ends = [feat_ref.at[pl.ds(part * size, size)] for part in range(2)]
-        feats.append(send_block(ends[0], row, 0, 2, beside, 0))
-        feats.append(send_block(ends[1], row, 1, 2, across, 2))
-        feats.append(send_block(ends[1], row, 1, 2, beside, 1))
-        feats.append(send_block(ends[0], row, 0, 2, across, 3))
-    else:
-        for step in range(1, rows):
-            feats.append(send_block(feat_ref, row, 0, 1, row_peer(step), step - 1))
-
     def pass_on():
         if passing:
             feats[0].wait_recv()
@@ -229,8 +229,11 @@
             feats[1].wait_recv()
             feats.append(send_block(gathered.at[block(across, 1, 2)], across, 1, 2, beside, 5))
 
-    branches[0, pl.ds(0, plan.lead), :] = jnp.zeros((plan.lead, 4 * own), BF16)
-    branches[rows - 1, pl.ds(plan.lead + tile, plan.lead), :] = jnp.zeros((plan.lead, 4 * own), BF16)
+    for half_number in range(2):
+        empty = jnp.zeros((plan.lead, 2 * own), BF16)
+        branches[half_number, 0, pl.ds(0, plan.lead), :] = empty
+        branches[half_number, rows - 1, pl.ds(plan.lead + tile, plan.lead), :] = empty
+    sums[...] = jnp.zeros(sums.shape, F32)
     distances = [rate // tc for rate in RATES]
     for number, far in enumerate(distances):
         @pl.when(col < far)
@@ -289,6 +292,68 @@
             def _():
                 copy.wait_send()
 
+    def multiply(owner, number):
+        for place, (which, tap) in enumerate(plan.taps):
+            if which != number:
+                continue
+            offset = (tap - 1) * RATES[number]
+            whole, rest = offset // plan.tr, offset % plan.tr
+            used = [whole, whole + 1] if rest else [whole]
+
+            def add(step, value):
+                to = owner - step
+
+                def body():
+                    sums[number, block(to), :] += value
+
+                if step == 0:
+                    body()
+                else:
+                    pl.when((to >= 0) & (to < rows))(body)
+
+            def body():
+                term = dot_t(gathered[block(owner), :], weights[place])
+                if rest:
+                    term = term.reshape(tile // plan.tr, plan.tr, 4 * own)
+                    term = pltpu.roll(term, plan.tr - rest, 1)
+                    upper = lax.broadcasted_iota(jnp.int32, term.shape, 1) < plan.tr - rest
+                    terms = [jnp.where(upper, term, 0.0), jnp.where(upper, 0.0, term)]
+                    terms = [value.reshape(tile, 4 * own) for value in terms]
+                else:
+                    terms = [term]
+                for step, value in zip(used, terms):
+                    add(step, value)
+
+            if offset == 0:
+                body()
+            else:
+                pl.when((owner - used[0] >= 0) & (owner - used[-1] < rows))(body)
+
+    def multiply_own():
+        copies["feat"].wait()
+        for name, copy in copies.items():
+            if name[0] == "tap":
+                copy.wait()
+        for number in range(3):
+            multiply(row, number)
+
+    if passing:
+        arrivals = [(beside, (2,)), (across, (3,)), (rows - 1 - row, (4, 5))]
+    else:
+        arrivals = [(lax.rem(row - step + rows, rows), (step - 1,)) for step in range(1, rows)]
+
+    def multiply_rest():
+        for owner, waits in arrivals[:-1]:
+            for at in waits:
+                feats[at].wait_recv()
+            for number in range(3):
+                multiply(owner, number)
+        for at in arrivals[-1][1]:
+            feats[at].wait_recv()
+
+    def last_products(number):
+        multiply(arrivals[-1][0], number)
+
     copies["low"].wait()
     reduced = dot_t(low_in[...], low_weight_ref[...]) + low_bias_ref[...]
     low_all[pl.ds(plan.lhalo, plan.fr * plan.fc), :] = jnp.maximum(reduced, 0.0).astype(BF16)
@@ -301,6 +366,7 @@
     )
     start_pair(low_rows)
 
+    multiply_own()
     pass_on()
     wait_recv_pair(low_rows)
     lsend[...] = dot(lpick_ref[:, pl.ds(0, plan.low)], low_all[pl.ds(0, plan.low), :]).astype(BF16)
@@ -315,8 +381,8 @@
 
     copies["proj"].wait()
     for w in range(rows):
-        for branch in range(4):
-            proj_blocks[w, pl.ds(branch * own, own), :] = proj[
+        for slot, branch in enumerate((0, 3, 1, 2)):
+            proj_blocks[w, pl.ds(slot * own, own), :] = proj[
                 pl.ds(branch * joined + w * own, own), :
             ]
 
@@ -345,44 +411,14 @@
             shifted[j - 1, pl.ds(0, hidden_px), :] = total
     low_part[...] += shifted[0, pl.ds(1, hidden_px), :] + shifted[1, pl.ds(2, hidden_px), :]
 
-    copies["feat"].wait()
-    for name, copy in copies.items():
-        if name[0] == "tap":
-            copy.wait()
-    for copy in feats[2 if passing else 0:]:
-        copy.wait_recv()
+    multiply_rest()
 
     half = plan.half
     sideways = [None, None, None]
     pool_copies = []
     for number in (2, 1, 0):
         rate = RATES[number]
-        for place, (which, tap) in enumerate(plan.taps):
-            if which == number and tap == 1:
-                sums[number] = dot_t(gathered[...], weights[place])
-        for place, (which, tap) in enumerate(plan.taps):
-            if which == number and tap != 1:
-                offset = (tap - 1) * rate
-                whole, rest = offset // plan.tr, offset % plan.tr
-                used = [whole, whole + 1] if rest else [whole]
-                first = max(0, used[0])
-                final = min(rows, rows + used[-1])
-                size = (final - first) * tile
-                term = dot_t(gathered[pl.ds(first * tile, size), :], weights[place])
-                if rest:
-                    term = term.reshape(size // plan.tr, plan.tr, 4 * own)
-                    term = pltpu.roll(term, plan.tr - rest, 1)
-                    upper = lax.broadcasted_iota(jnp.int32, term.shape, 1) < plan.tr - rest
-                    terms = [jnp.where(upper, term, 0.0), jnp.where(upper, 0.0, term)]
-                    terms = [value.reshape(size, 4 * own) for value in terms]
-                else:
-                    terms = [term]
-                for step, value in zip(used, terms):
-                    begin, end = max(0, -step), min(rows, rows - step)
-                    count = (end - begin) * tile
-                    if count > 0:
-                        skip = (begin + step - first) * tile
-                        sums[number, pl.ds(begin * tile, count), :] += value[skip:skip + count]
+        last_products(number)
         for side in range(2):
             lanes = pl.ds(side * own, own)
             zsend[number, side] = jnp.concatenate(
@@ -414,6 +450,51 @@
                 )
                 copy.start()
                 pool_copies.append(copy)
+
+    def bias(number):
+        return aspp_bias_ref[pl.ds(number, 1), :]
+
+    def point_branch(part):
+        value = sums[0, pl.ds(part * half, half), pl.ds(3 * own, own)]
+        return jnp.maximum(value + bias(0), 0.0).astype(BF16)
+
+    def arrive(number):
+        for there, come, copy in sideways[number]:
+            @pl.when(come)
+            def _():
+                copy.wait_recv()
+
+    def atrous_branch(number, part):
+        lanes = pl.ds(part * own, own)
+        value = sums[number, pl.ds(part * half, half), pl.ds(2 * own, own)]
+        value = value + zrecv[number, 0, :, lanes].astype(F32) + zrecv[number, 1, :, lanes].astype(F32)
+        return jnp.maximum(value + bias(number + 1), 0.0).astype(BF16)
+
+    b_copies = [[], []]
+
+    def send_branches(message, made):
+        joint = [jnp.concatenate(made(part), axis=1) for part in range(2)]
+        joint = jnp.concatenate(joint, axis=0)
+        for place in range(rows):
+            value = joint[place * tile:(place + 1) * tile]
+            branches[message, place, pl.ds(plan.lead, tile), :] = value
+            ends = dot(rpick_ref[:, pl.ds(0, tile)], value).astype(BF16)
+            if place + 1 < rows:
+                branches[message, place + 1, pl.ds(0, plan.lead), :] = ends[: plan.lead]
+            if place > 0:
+                branches[message, place - 1, pl.ds(plan.lead + tile, plan.lead), :] = ends[plan.lead:]
+        for step in range(1, rows):
+            copy = pltpu.make_async_remote_copy(
+                src_ref=branches.at[message, row_peer(step)], dst_ref=brecv.at[message, row],
+                send_sem=b_send.at[message, step - 1], recv_sem=b_recv.at[message, step - 1],
+                device_id=(dp, row_peer(step), col), device_id_type=MESH,
+            )
+            copy.start()
+            b_copies[message].append(copy)
+        brecv[message, row] = branches[message, row]
+
+    arrive(2)
+    send_branches(0, lambda part: [point_branch(part), atrous_branch(2, part)])
 
     for copy in pool_copies:
         copy.wait_recv()
@@ -433,45 +514,9 @@
         copy.start()
         bp_copies.append(copy)
 
-    def bias(number):
-        return aspp_bias_ref[pl.ds(number, 1), :]
-
-    halves = []
-    for part in range(2):
-        at = pl.ds(part * half, half)
-        halves.append([jnp.maximum(sums[0, at, pl.ds(3 * own, own)] + bias(0), 0.0).astype(BF16)])
-    for number in (2, 1, 0):
-        for side, (there, come, copy) in enumerate(sideways[number]):
-            @pl.when(come)
-            def _():
-                copy.wait_recv()
-    for number in range(3):
-        arrived = zrecv[number, 0].astype(F32) + zrecv[number, 1].astype(F32)
-        for part in range(2):
-            at = pl.ds(part * half, half)
-            value = sums[number, at, pl.ds(2 * own, own)] + arrived[:, part * own:(part + 1) * own]
-            halves[part].append(jnp.maximum(value + bias(number + 1), 0.0).astype(BF16))
-    joint = [jnp.concatenate(halves[part], axis=1) for part in range(2)]
-    joint = jnp.concatenate(joint, axis=0)
-    for place in range(rows):
-        value = joint[place * tile:(place + 1) * tile]
-        branches[place, pl.ds(plan.lead, tile), :] = value
-        ends = dot(rpick_ref[:, pl.ds(0, tile)], value).astype(BF16)
-        if place + 1 < rows:
-            branches[place + 1, pl.ds(0, plan.lead), :] = ends[: plan.lead]
-        if place > 0:
-            branches[place - 1, pl.ds(plan.lead + tile, plan.lead), :] = ends[plan.lead:]
-
-    b_copies = []
-    for step in range(1, rows):
-        copy = pltpu.make_async_remote_copy(
-            src_ref=branches.at[row_peer(step)], dst_ref=brecv.at[row],
-            send_sem=b_send.at[step - 1], recv_sem=b_recv.at[step - 1],
-            device_id=(dp, row_peer(step), col), device_id_type=MESH,
-        )
-        copy.start()
-        b_copies.append(copy)
-    brecv[row] = branches[row]
+    arrive(1)
+    arrive(0)
+    send_branches(1, lambda part: [atrous_branch(0, part), atrous_branch(1, part)])
 
     for copy in bp_copies:
         copy.wait_recv()
@@ -480,11 +525,14 @@
         constant = constant + dot(
             branch_pool[w], proj[pl.ds(4 * joined + w * own, own), :]
         )[0:1, :]
-    for copy in b_copies:
-        copy.wait_recv()
     coarse = constant
-    for w in range(rows):
-        coarse = coarse + dot(brecv[w], proj_blocks[w])
+    for message in range(2):
+        for copy in b_copies[message]:
+            copy.wait_recv()
+        for w in range(rows):
+            coarse = coarse + dot(
+                brecv[message, w], proj_blocks[w, pl.ds(message * 2 * own, 2 * own), :]
+            )
     coarse = jnp.maximum(coarse, 0.0).astype(BF16)
 
     cstrips[...] = dot(cpick_ref[:, pl.ds(0, plan.span)], coarse).astype(BF16)
@@ -536,7 +584,7 @@
     result = jnp.maximum(result, 0.0).reshape(plan.fr, width, wide)
     out_ref[...] = result[:, : plan.fc, :].astype(BF16)
 
-    for copy in feats + pool_copies + bp_copies + b_copies:
+    for copy in feats + pool_copies + bp_copies + b_copies[0] + b_copies[1]:
         copy.wait_send()
     for made in sideways:
         for there, come, copy in made:
@@ -579,8 +627,8 @@
         pltpu.VMEM((3, 2, plan.half, 2 * own), BF16),
         pltpu.VMEM((cols, 8, own), F32),
         pltpu.VMEM((rows, 16, own), BF16),
-        pltpu.VMEM((rows, plan.span, 4 * own), BF16),
-        pltpu.VMEM((rows, plan.span, 4 * own), BF16),
+        pltpu.VMEM((2, rows, plan.span, 2 * own), BF16),
+        pltpu.VMEM((2, rows, plan.span, 2 * own), BF16),
         pltpu.VMEM((rows, 4 * own, out_width), BF16),
         pltpu.VMEM((2 * plan.cstrip, out_width), BF16),
         pltpu.VMEM((2, plan.cstrip, out_width), BF16),
@@ -596,7 +644,7 @@
         dma((3, 2)), dma((3, 2)),
         dma((cols - 1,)), dma((cols - 1,)),
         dma((rows - 1,)), dma((rows - 1,)),
-        dma((rows - 1,)), dma((rows - 1,)),
+        dma((2, rows - 1)), dma((2, rows - 1)),
         dma((2,)), dma((2,)), dma((2,)), dma((2,)), dma((2,)), dma((2,)),
     ]
     return pl.pallas_call(

time: 44.1 us -> 45.9 us (1.041)
  Pallas kernels: 42.4 us -> 44.1 us
    pallas_call x1, Pallas kernels: 42.4 us -> 44.1 us  [on_device(): pl.pallas_call(functools.partial(kernel, plan), out_shape=jax.ShapeDtypeS...]
where the time goes in v3:
time: 45.9 us; the launch traced here: 45.7 us
  Pallas kernels  44.1 us (96%)
  local copies, waits for them, and re-layouts  1.62 us (4%)
    pallas_call x1, Pallas kernels, on_device(): pl.pallas_call(functools.partial(kernel, plan), out_shape=jax.ShapeDtypeS...  44.1 us
    unnamed x1, local copies, waits for them, and re-layouts  1.62 us

profile of v3, /device:TPU:0, one launch (start us, length us, event | category | flops | bytes accessed | tf_op | source)
XLA Modules:
  0.0 45.7 jit_solution(7552101820402504567)
XLA Ops:
  0.0 44.1 %shard_map.190 = bf16[16,24,256]{2,1,0:T(8,128)(2,1)} custom-call(bf16[96,2048]{1,0:T(8,128)(2,1)} %bitcast.13, bf16[384,256]{1,0:T(8,128)(2,1)} %bitcast.16, bf16[64,2048]{1,0:T(8,128)(2,1)} %bitcast.14, bf16[3,3,3,64,2048]{4,3,2,1,0:T(8,128)(2,1)} %bitcast.12, bf16[64,2048]{1,0:T(8,128)(2,1)} %bitcast.15, f32[5,64]{1,0:T(8,128)} %aspp_bias_ref.1, ...), custom_call_target="tpu_custom_call" | custom-call | tf_op jit(solution)/shard_map/pallas_call | solution.py:650
  44.1 1.6 %copy.22 = bf16[16,24,256]{2,1,0:T(8,128)(2,1)} copy(bf16[16,24,256]{2,1,0:T(8,128)(2,1)} %shard_map.190) | data formatting | bytes 393216

commit v4 on v3

--- a/solution.py
+++ b/solution.py
@@ -139,7 +139,7 @@
     low_weight_ref, low_bias_ref, conv1_ref, conv1_bias_ref, conv2_ref, conv2_bias_ref,
     up_own_ref, up_side_ref, rpick_ref, cpick_ref, lpick_ref, lwindow_ref,
     out_ref,
-    gathered, weights, low_in, proj, conv1, conv2, up_own, up_side, lwindow,
+    gathered, weights, turned, low_in, proj, conv1, conv2, up_own, up_side, lwindow,
     sums, zsend, zrecv, pools, branch_pool, branches, brecv, proj_blocks,
     cstrips, crecv, low_all, lsend, reduced_window, shifted, low_part, up_window, hidden,
     local_sem, feat_send, feat_recv, z_send, z_recv, pool_send, pool_recv, bp_send, bp_recv,
@@ -233,7 +233,6 @@
         empty = jnp.zeros((plan.lead, 2 * own), BF16)
         branches[half_number, 0, pl.ds(0, plan.lead), :] = empty
         branches[half_number, rows - 1, pl.ds(plan.lead + tile, plan.lead), :] = empty
-    sums[...] = jnp.zeros(sums.shape, F32)
     distances = [rate // tc for rate in RATES]
     for number, far in enumerate(distances):
         @pl.when(col < far)
@@ -292,67 +291,43 @@
             def _():
                 copy.wait_send()
 
-    def multiply(owner, number):
+    piece = min(256, depth)
+
+    def turn_weights():
+        for name, copy in copies.items():
+            if name[0] == "tap":
+                copy.wait()
+        for place in range(len(plan.taps)):
+            for begin in range(0, depth, piece):
+                turned[place, pl.ds(begin, piece), :] = weights[place, :, pl.ds(begin, piece)].T
+
+    def products(number):
         for place, (which, tap) in enumerate(plan.taps):
-            if which != number:
-                continue
-            offset = (tap - 1) * RATES[number]
-            whole, rest = offset // plan.tr, offset % plan.tr
-            used = [whole, whole + 1] if rest else [whole]
-
-            def add(step, value):
-                to = owner - step
-
-                def body():
-                    sums[number, block(to), :] += value
-
-                if step == 0:
-                    body()
-                else:
-                    pl.when((to >= 0) & (to < rows))(body)
-
-            def body():
-                term = dot_t(gathered[block(owner), :], weights[place])
+            if which == number and tap == 1:
+                sums[number] = dot(gathered[...], turned[place])
+        for place, (which, tap) in enumerate(plan.taps):
+            if which == number and tap != 1:
+                offset = (tap - 1) * RATES[number]
+                whole, rest = offset // plan.tr, offset % plan.tr
+                used = [whole, whole + 1] if rest else [whole]
+                first = max(0, used[0])
+                final = min(rows, rows + used[-1])
+                size = (final - first) * tile
+                term = dot(gathered[pl.ds(first * tile, size), :], turned[place])
                 if rest:
-                    term = term.reshape(tile // plan.tr, plan.tr, 4 * own)
+                    term = term.reshape(size // plan.tr, plan.tr, 4 * own)
                     term = pltpu.roll(term, plan.tr - rest, 1)
                     upper = lax.broadcasted_iota(jnp.int32, term.shape, 1) < plan.tr - rest
                     terms = [jnp.where(upper, term, 0.0), jnp.where(upper, 0.0, term)]
-                    terms = [value.reshape(tile, 4 * own) for value in terms]
+                    terms = [value.reshape(size, 4 * own) for value in terms]
                 else:
                     terms = [term]
                 for step, value in zip(used, terms):
-                    add(step, value)
-
-            if offset == 0:
-                body()
-            else:
-                pl.when((owner - used[0] >= 0) & (owner - used[-1] < rows))(body)
-
-    def multiply_own():
-        copies["feat"].wait()
-        for name, copy in copies.items():
-            if name[0] == "tap":
-                copy.wait()
-        for number in range(3):
-            multiply(row, number)
-
-    if passing:
-        arrivals = [(beside, (2,)), (across, (3,)), (rows - 1 - row, (4, 5))]
-    else:
-        arrivals = [(lax.rem(row - step + rows, rows), (step - 1,)) for step in range(1, rows)]
-
-    def multiply_rest():
-        for owner, waits in arrivals[:-1]:
-            for at in waits:
-                feats[at].wait_recv()
-            for number in range(3):
-                multiply(owner, number)
-        for at in arrivals[-1][1]:
-            feats[at].wait_recv()
-
-    def last_products(number):
-        multiply(arrivals[-1][0], number)
+                    begin, end = max(0, -step), min(rows, rows - step)
+                    count = (end - begin) * tile
+                    if count > 0:
+                        skip = (begin + step - first) * tile
+                        sums[number, pl.ds(begin * tile, count), :] += value[skip:skip + count]
 
     copies["low"].wait()
     reduced = dot_t(low_in[...], low_weight_ref[...]) + low_bias_ref[...]
@@ -366,7 +341,7 @@
     )
     start_pair(low_rows)
 
-    multiply_own()
+    turn_weights()
     pass_on()
     wait_recv_pair(low_rows)
     lsend[...] = dot(lpick_ref[:, pl.ds(0, plan.low)], low_all[pl.ds(0, plan.low), :]).astype(BF16)
@@ -411,14 +386,16 @@
             shifted[j - 1, pl.ds(0, hidden_px), :] = total
     low_part[...] += shifted[0, pl.ds(1, hidden_px), :] + shifted[1, pl.ds(2, hidden_px), :]
 
-    multiply_rest()
+    copies["feat"].wait()
+    for copy in feats[2 if passing else 0:]:
+        copy.wait_recv()
 
     half = plan.half
     sideways = [None, None, None]
     pool_copies = []
     for number in (2, 1, 0):
         rate = RATES[number]
-        last_products(number)
+        products(number)
         for side in range(2):
             lanes = pl.ds(side * own, own)
             zsend[number, side] = jnp.concatenate(
@@ -615,6 +592,7 @@
     scratch = [
         pltpu.VMEM((plan.pixels, depth), BF16),
         pltpu.VMEM((taps, 4 * own, depth), BF16),
+        pltpu.VMEM((taps, depth, 4 * own), BF16),
         pltpu.VMEM((plan.fr * plan.fc, low_level.shape[2]), BF16),
         pltpu.VMEM(proj_weight.shape, BF16),
         pltpu.VMEM(conv1_weight.shape, BF16),

time: 45.9 us -> 42.5 us (0.926)
  Pallas kernels: 44.1 us -> 40.7 us
    pallas_call x1, Pallas kernels: 44.1 us -> 40.7 us  [on_device(): pl.pallas_call(functools.partial(kernel, plan), out_shape=jax.ShapeDtypeS...]
where the time goes in v4:
time: 42.5 us; the launch traced here: 42.4 us
  Pallas kernels  40.7 us (96%)
  local copies, waits for them, and re-layouts  1.62 us (4%)
    pallas_call x1, Pallas kernels, on_device(): pl.pallas_call(functools.partial(kernel, plan), out_shape=jax.ShapeDtypeS...  40.7 us
    unnamed x1, local copies, waits for them, and re-layouts  1.62 us

profile of v4, /device:TPU:0, one launch (start us, length us, event | category | flops | bytes accessed | tf_op | source)
XLA Modules:
  0.0 42.4 jit_solution(6393619565920169273)
XLA Ops:
  0.0 40.7 %shard_map.190 = bf16[16,24,256]{2,1,0:T(8,128)(2,1)} custom-call(bf16[96,2048]{1,0:T(8,128)(2,1)} %bitcast.13, bf16[384,256]{1,0:T(8,128)(2,1)} %bitcast.16, bf16[64,2048]{1,0:T(8,128)(2,1)} %bitcast.14, bf16[3,3,3,64,2048]{4,3,2,1,0:T(8,128)(2,1)} %bitcast.12, bf16[64,2048]{1,0:T(8,128)(2,1)} %bitcast.15, f32[5,64]{1,0:T(8,128)} %aspp_bias_ref.1, ...), custom_call_target="tpu_custom_call" | custom-call | tf_op jit(solution)/shard_map/pallas_call | solution.py:628
  40.8 1.6 %copy.22 = bf16[16,24,256]{2,1,0:T(8,128)(2,1)} copy(bf16[16,24,256]{2,1,0:T(8,128)(2,1)} %shard_map.190) | data formatting | bytes 393216

commit v5 on v4

--- a/solution.py
+++ b/solution.py
@@ -29,10 +29,12 @@
         self.tr, self.tc = tile_rows, tile_cols
         self.tile = tile_rows * tile_cols
         self.height = rows * tile_rows
-        self.pixels = self.height * tile_cols
+        self.pc = tile_cols // 2
+        self.pt = self.pc * tile_rows
+        self.pixels = rows * self.pt
         self.half = self.pixels // 2
-        self.lead = up16(2 * tile_cols)
-        self.span = self.tile + 2 * self.lead
+        self.lead = up16(2 * self.pc)
+        self.span = self.pt + 2 * self.lead
         self.cstrip = up16((tile_rows + 4) * 2)
         self.fr, self.fc = 2 * tile_rows, 2 * tile_cols
         self.wr, self.wc = self.fr + 4, self.fc + 4
@@ -48,7 +50,7 @@
                     self.taps.append((number, tap))
 
     def upsample(self):
-        own = np.zeros((9, self.window, self.span), np.float32)
+        own = np.zeros((9, self.window, 2 * self.span), np.float32)
         side = np.zeros((9, self.window, 2 * self.cstrip), np.float32)
 
         def terms(fine, length, first, last):
@@ -80,22 +82,23 @@
         return table(own), table(side)
 
     def pixel(self, y, x):
+        base, x = (x // self.pc) * self.span, x % self.pc
         if y < 0:
-            return x * 2 + y + 2
+            return base + x * 2 + y + 2
         if y >= self.tr:
-            return self.lead + self.tile + x * 2 + y - self.tr
-        return self.lead + x * self.tr + y
+            return base + self.lead + self.pt + x * 2 + y - self.tr
+        return base + self.lead + x * self.tr + y
 
     def row_strips(self):
-        pick = np.zeros((2 * self.lead, self.tile), np.float32)
-        for x in range(self.tc):
+        pick = np.zeros((2 * self.lead, self.pt), np.float32)
+        for x in range(self.pc):
             for y in range(2):
                 pick[x * 2 + y, x * self.tr + self.tr - 2 + y] = 1
                 pick[self.lead + x * 2 + y, x * self.tr + y] = 1
         return table(pick)
 
     def coarse_strips(self):
-        pick = np.zeros((2 * self.cstrip, self.span), np.float32)
+        pick = np.zeros((2 * self.cstrip, 2 * self.span), np.float32)
         for y in range(-2, self.tr + 2):
             for x in range(2):
                 pick[(y + 2) * 2 + x, self.pixel(y, x)] = 1
@@ -164,38 +167,60 @@
         pl.semaphore_signal(barrier, inc=1, device_id=(dp, row, col_peer(step)), device_id_type=MESH)
     pl.semaphore_wait(barrier, rows + cols - 2)
 
-    def block(owner, part=0, parts=1):
-        size = tile // parts
-        return pl.ds(pl.multiple_of(owner * tile + part * size, 16), size)
-
-    def send_block(src, owner, part, parts, target, at):
+    pt = plan.pt
+
+    def block(owner, begin=0, size=pt):
+        return pl.ds(pl.multiple_of(owner * pt + begin, 16), size)
+
+    def send_block(src, owner, half_tile, begin, size, target, at):
         copy = pltpu.make_async_remote_copy(
-            src_ref=src, dst_ref=gathered.at[block(owner, part, parts)],
-            send_sem=feat_send.at[at], recv_sem=feat_recv.at[at],
+            src_ref=src, dst_ref=gathered.at[half_tile, block(owner, begin, size)],
+            send_sem=feat_send.at[half_tile, at], recv_sem=feat_recv.at[half_tile, at],
             device_id=(dp, target, col), device_id_type=MESH,
         )
         copy.start()
         return copy
 
-    feats = []
+    feats = [[], []]
     passing = rows == 4
     if passing:
         beside = row + 1 - 2 * lax.rem(row, 2)
         across = row + 2 - 4 * (row // 2)
-        size = tile // 2
-        ends = [feat_ref.at[pl.ds(part * size, size)] for part in range(2)]
-        feats.append(send_block(ends[0], row, 0, 2, beside, 0))
-        feats.append(send_block(ends[1], row, 1, 2, across, 2))
-        feats.append(send_block(ends[1], row, 1, 2, beside, 1))
-        feats.append(send_block(ends[0], row, 0, 2, across, 3))
-    else:
-        for step in range(1, rows):
-            feats.append(send_block(feat_ref, row, 0, 1, row_peer(step), step - 1))
+    longer = up16(pt // 2)
+    ranges = [((0, longer), (longer, pt - longer)), ((0, pt - longer), (pt - longer, longer))]
+
+    def send_features(half_tile):
+        made = feats[half_tile]
+        if passing:
+            ends = [feat_ref.at[pl.ds(half_tile * pt + begin, size)] for begin, size in ranges[half_tile]]
+            for number, target, at in ((0, beside, 0), (1, across, 2), (1, beside, 1), (0, across, 3)):
+                made.append(send_block(ends[number], row, half_tile, *ranges[half_tile][number], target, at))
+        else:
+            src = feat_ref.at[pl.ds(half_tile * pt, pt)]
+            for step in range(1, rows):
+                made.append(send_block(src, row, half_tile, 0, pt, row_peer(step), step - 1))
+
+    def pass_on(half_tile):
+        if passing:
+            made = feats[half_tile]
+            for number, source, target, at in ((0, beside, across, 4), (1, across, beside, 5)):
+                made[number].wait_recv()
+                begin, size = ranges[half_tile][number]
+                src = gathered.at[half_tile, block(source, begin, size)]
+                made.append(send_block(src, source, half_tile, begin, size, target, at))
+
+    def wait_features(half_tile):
+        copies["feat%d" % half_tile].wait()
+        for copy in feats[half_tile][2 if passing else 0:]:
+            copy.wait_recv()
+
+    send_features(0)
 
     copies = {}
     numbered = [
         ("low", low_ref, low_in),
-        ("feat", feat_ref, gathered.at[pl.ds(pl.multiple_of(row * tile, 16), tile)]),
+        ("feat0", feat_ref.at[pl.ds(0, pt)], gathered.at[0, block(row)]),
+        ("feat1", feat_ref.at[pl.ds(pt, pt)], gathered.at[1, block(row)]),
         ("proj", proj_ref, proj),
         ("conv1", conv1_ref, conv1),
         ("conv2", conv2_ref, conv2),
@@ -222,26 +247,21 @@
         copies[name] = pltpu.make_async_copy(src, dst, local_sem.at[place])
         copies[name].start()
 
-    def pass_on():
-        if passing:
-            feats[0].wait_recv()
-            feats.append(send_block(gathered.at[block(beside, 0, 2)], beside, 0, 2, across, 4))
-            feats[1].wait_recv()
-            feats.append(send_block(gathered.at[block(across, 1, 2)], across, 1, 2, beside, 5))
-
     for half_number in range(2):
-        empty = jnp.zeros((plan.lead, 2 * own), BF16)
+        empty = jnp.zeros((plan.lead, 4 * own), BF16)
         branches[half_number, 0, pl.ds(0, plan.lead), :] = empty
-        branches[half_number, rows - 1, pl.ds(plan.lead + tile, plan.lead), :] = empty
+        branches[half_number, rows - 1, pl.ds(plan.lead + pt, plan.lead), :] = empty
     distances = [rate // tc for rate in RATES]
     for number, far in enumerate(distances):
         @pl.when(col < far)
         def _():
-            zrecv[number, 0] = jnp.zeros(zrecv.shape[2:], BF16)
+            for half_tile in range(2):
+                zrecv[half_tile, number, 0] = jnp.zeros(zrecv.shape[3:], BF16)
 
         @pl.when(col + far >= cols)
         def _():
-            zrecv[number, 1] = jnp.zeros(zrecv.shape[2:], BF16)
+            for half_tile in range(2):
+                zrecv[half_tile, number, 1] = jnp.zeros(zrecv.shape[3:], BF16)
 
     low_ends = (pl.ds(0, plan.lhalo), pl.ds(plan.low - plan.lhalo, plan.lhalo))
     low_sides = (pl.ds(plan.low, plan.lstrip), pl.ds(plan.low + plan.lstrip, plan.lstrip))
@@ -301,10 +321,10 @@
             for begin in range(0, depth, piece):
                 turned[place, pl.ds(begin, piece), :] = weights[place, :, pl.ds(begin, piece)].T
 
-    def products(number):
+    def products(half_tile, number):
         for place, (which, tap) in enumerate(plan.taps):
             if which == number and tap == 1:
-                sums[number] = dot(gathered[...], turned[place])
+                sums[half_tile, number] = dot(gathered[half_tile], turned[place])
         for place, (which, tap) in enumerate(plan.taps):
             if which == number and tap != 1:
                 offset = (tap - 1) * RATES[number]
@@ -312,8 +332,8 @@
                 used = [whole, whole + 1] if rest else [whole]
                 first = max(0, used[0])
                 final = min(rows, rows + used[-1])
-                size = (final - first) * tile
-                term = dot(gathered[pl.ds(first * tile, size), :], turned[place])
+                size = (final - first) * pt
+                term = dot(gathered[half_tile, pl.ds(first * pt, size), :], turned[place])
                 if rest:
                     term = term.reshape(size // plan.tr, plan.tr, 4 * own)
                     term = pltpu.roll(term, plan.tr - rest, 1)
@@ -324,10 +344,10 @@
                     terms = [term]
                 for step, value in zip(used, terms):
                     begin, end = max(0, -step), min(rows, rows - step)
-                    count = (end - begin) * tile
+                    count = (end - begin) * pt
                     if count > 0:
-                        skip = (begin + step - first) * tile
-                        sums[number, pl.ds(begin * tile, count), :] += value[skip:skip + count]
+                        skip = (begin + step - first) * pt
+                        sums[half_tile, number, pl.ds(begin * pt, count), :] += value[skip:skip + count]
 
     copies["low"].wait()
     reduced = dot_t(low_in[...], low_weight_ref[...]) + low_bias_ref[...]
@@ -341,8 +361,101 @@
     )
     start_pair(low_rows)
 
+    half = plan.half
+    sideways = [[None] * 3, [None] * 3]
+    pool_copies = []
+
+    def spread(half_tile, number):
+        for side in range(2):
+            lanes = pl.ds(side * own, own)
+            zsend[half_tile, number, side] = jnp.concatenate(
+                [sums[half_tile, number, pl.ds(part * half, half), lanes] for part in range(2)], axis=1
+            ).astype(BF16)
+        made = []
+        for side, far in ((0, distances[number]), (1, -distances[number])):
+            there = col + far < cols if far > 0 else col + far >= 0
+            come = col - far < cols if far < 0 else col - far >= 0
+            copy = pltpu.make_async_remote_copy(
+                src_ref=zsend.at[half_tile, number, side], dst_ref=zrecv.at[half_tile, number, side],
+                send_sem=z_send.at[half_tile, number, side], recv_sem=z_recv.at[half_tile, number, side],
+                device_id=(dp, row, lax.rem(col + far + 4 * cols, cols)), device_id_type=MESH,
+            )
+            made.append((there, come, copy))
+
+            @pl.when(there)
+            def _():
+                copy.start()
+        sideways[half_tile][number] = made
+
+    def spread_pool():
+        part = sum(
+            jnp.sum(sums[half_tile, 1, :, pl.ds(3 * own, own)], axis=0, keepdims=True)
+            for half_tile in range(2)
+        )
+        pools[col] = jnp.broadcast_to(part, (8, own))
+        for step in range(1, cols):
+            copy = pltpu.make_async_remote_copy(
+                src_ref=pools.at[col], dst_ref=pools.at[col],
+                send_sem=pool_send.at[step - 1], recv_sem=pool_recv.at[step - 1],
+                device_id=(dp, row, col_peer(step)), device_id_type=MESH,
+            )
+            copy.start()
+            pool_copies.append(copy)
+
+    def bias(number):
+        return aspp_bias_ref[pl.ds(number, 1), :]
+
+    def point_branch(half_tile, part):
+        value = sums[half_tile, 0, pl.ds(part * half, half), pl.ds(3 * own, own)]
+        return jnp.maximum(value + bias(0), 0.0).astype(BF16)
+
+    def atrous_branch(half_tile, number, part):
+        lanes = pl.ds(part * own, own)
+        value = sums[half_tile, number, pl.ds(part * half, half), pl.ds(2 * own, own)]
+        for side in range(2):
+            value = value + zrecv[half_tile, number, side, :, lanes].astype(F32)
+        return jnp.maximum(value + bias(number + 1), 0.0).astype(BF16)
+
+    b_copies = [[], []]
+
+    def send_branches(half_tile):
+        for number in (2, 1, 0):
+            for there, come, copy in sideways[half_tile][number]:
+                @pl.when(come)
+                def _():
+                    copy.wait_recv()
+        joint = []
+        for part in range(2):
+            made = [point_branch(half_tile, part)]
+            made += [atrous_branch(half_tile, number, part) for number in range(3)]
+            joint.append(jnp.concatenate(made, axis=1))
+        joint = jnp.concatenate(joint, axis=0)
+        for place in range(rows):
+            value = joint[place * pt:(place + 1) * pt]
+            branches[half_tile, place, pl.ds(plan.lead, pt), :] = value
+            ends = dot(rpick_ref[:, pl.ds(0, pt)], value).astype(BF16)
+            if place + 1 < rows:
+                branches[half_tile, place + 1, pl.ds(0, plan.lead), :] = ends[: plan.lead]
+            if place > 0:
+                branches[half_tile, place - 1, pl.ds(plan.lead + pt, plan.lead), :] = ends[plan.lead:]
+        for step in range(1, rows):
+            copy = pltpu.make_async_remote_copy(
+                src_ref=branches.at[half_tile, row_peer(step)], dst_ref=brecv.at[half_tile, row],
+                send_sem=b_send.at[half_tile, step - 1], recv_sem=b_recv.at[half_tile, step - 1],
+                device_id=(dp, row_peer(step), col), device_id_type=MESH,
+            )
+            copy.start()
+            b_copies[half_tile].append(copy)
+        brecv[half_tile, row] = branches[half_tile, row]
+
+    pass_on(0)
+    send_features(1)
     turn_weights()
-    pass_on()
+    wait_features(0)
+    for number in (2, 1, 0):
+        products(0, number)
+        spread(0, number)
+    pass_on(1)
     wait_recv_pair(low_rows)
     lsend[...] = dot(lpick_ref[:, pl.ds(0, plan.low)], low_all[pl.ds(0, plan.low), :]).astype(BF16)
     low_cols = pair(
@@ -356,8 +469,8 @@
 
     copies["proj"].wait()
     for w in range(rows):
-        for slot, branch in enumerate((0, 3, 1, 2)):
-            proj_blocks[w, pl.ds(slot * own, own), :] = proj[
+        for branch in range(4):
+            proj_blocks[w, pl.ds(branch * own, own), :] = proj[
                 pl.ds(branch * joined + w * own, own), :
             ]
 
@@ -386,92 +499,13 @@
             shifted[j - 1, pl.ds(0, hidden_px), :] = total
     low_part[...] += shifted[0, pl.ds(1, hidden_px), :] + shifted[1, pl.ds(2, hidden_px), :]
 
-    copies["feat"].wait()
-    for copy in feats[2 if passing else 0:]:
-        copy.wait_recv()
-
-    half = plan.half
-    sideways = [None, None, None]
-    pool_copies = []
+    send_branches(0)
+    wait_features(1)
     for number in (2, 1, 0):
-        rate = RATES[number]
-        products(number)
-        for side in range(2):
-            lanes = pl.ds(side * own, own)
-            zsend[number, side] = jnp.concatenate(
-                [sums[number, pl.ds(0, half), lanes], sums[number, pl.ds(half, half), lanes]], axis=1
-            ).astype(BF16)
-        made = []
-        for side, far in ((0, distances[number]), (1, -distances[number])):
-            there = col + far < cols if far > 0 else col + far >= 0
-            come = col - far < cols if far < 0 else col - far >= 0
-            copy = pltpu.make_async_remote_copy(
-                src_ref=zsend.at[number, side], dst_ref=zrecv.at[number, side],
-                send_sem=z_send.at[number, side], recv_sem=z_recv.at[number, side],
-                device_id=(dp, row, lax.rem(col + far + 4 * cols, cols)), device_id_type=MESH,
-            )
-            made.append((there, come, copy))
-
-            @pl.when(there)
-            def _():
-                copy.start()
-        sideways[number] = made
+        products(1, number)
+        spread(1, number)
         if number == 1:
-            part = jnp.sum(sums[number, :, pl.ds(3 * own, own)], axis=0, keepdims=True)
-            pools[col] = jnp.broadcast_to(part, (8, own))
-            for step in range(1, cols):
-                copy = pltpu.make_async_remote_copy(
-                    src_ref=pools.at[col], dst_ref=pools.at[col],
-                    send_sem=pool_send.at[step - 1], recv_sem=pool_recv.at[step - 1],
-                    device_id=(dp, row, col_peer(step)), device_id_type=MESH,
-                )
-                copy.start()
-                pool_copies.append(copy)
-
-    def bias(number):
-        return aspp_bias_ref[pl.ds(number, 1), :]
-
-    def point_branch(part):
-        value = sums[0, pl.ds(part * half, half), pl.ds(3 * own, own)]
-        return jnp.maximum(value + bias(0), 0.0).astype(BF16)
-
-    def arrive(number):
-        for there, come, copy in sideways[number]:
-            @pl.when(come)
-            def _():
-                copy.wait_recv()
-
-    def atrous_branch(number, part):
-        lanes = pl.ds(part * own, own)
-        value = sums[number, pl.ds(part * half, half), pl.ds(2 * own, own)]
-        value = value + zrecv[number, 0, :, lanes].astype(F32) + zrecv[number, 1, :, lanes].astype(F32)
-        return jnp.maximum(value + bias(number + 1), 0.0).astype(BF16)
-
-    b_copies = [[], []]
-
-    def send_branches(message, made):
-        joint = [jnp.concatenate(made(part), axis=1) for part in range(2)]
-        joint = jnp.concatenate(joint, axis=0)
-        for place in range(rows):
-            value = joint[place * tile:(place + 1) * tile]
-            branches[message, place, pl.ds(plan.lead, tile), :] = value
-            ends = dot(rpick_ref[:, pl.ds(0, tile)], value).astype(BF16)
-            if place + 1 < rows:
-                branches[message, place + 1, pl.ds(0, plan.lead), :] = ends[: plan.lead]
-            if place > 0:
-                branches[message, place - 1, pl.ds(plan.lead + tile, plan.lead), :] = ends[plan.lead:]
-        for step in range(1, rows):
-            copy = pltpu.make_async_remote_copy(
-                src_ref=branches.at[message, row_peer(step)], dst_ref=brecv.at[message, row],
-                send_sem=b_send.at[message, step - 1], recv_sem=b_recv.at[message, step - 1],
-                device_id=(dp, row_peer(step), col), device_id_type=MESH,
-            )
-            copy.start()
-            b_copies[message].append(copy)
-        brecv[message, row] = branches[message, row]
-
-    arrive(2)
-    send_branches(0, lambda part: [point_branch(part), atrous_branch(2, part)])
+            spread_pool()
 
     for copy in pool_copies:
         copy.wait_recv()
@@ -491,10 +525,7 @@
         copy.start()
         bp_copies.append(copy)
 
-    arrive(1)
-    arrive(0)
-    send_branches(1, lambda part: [atrous_branch(0, part), atrous_branch(1, part)])
-
+    send_branches(1)
     for copy in bp_copies:
         copy.wait_recv()
     constant = proj_bias_ref[...]
@@ -502,17 +533,18 @@
         constant = constant + dot(
             branch_pool[w], proj[pl.ds(4 * joined + w * own, own), :]
         )[0:1, :]
-    coarse = constant
-    for message in range(2):
-        for copy in b_copies[message]:
+    coarse = []
+    for half_tile in range(2):
+        for copy in b_copies[half_tile]:
             copy.wait_recv()
+        total = constant
         for w in range(rows):
-            coarse = coarse + dot(
-                brecv[message, w], proj_blocks[w, pl.ds(message * 2 * own, 2 * own), :]
-            )
+            total = total + dot(brecv[half_tile, w], proj_blocks[w])
+        coarse.append(total)
+    coarse = jnp.concatenate(coarse, axis=0)
     coarse = jnp.maximum(coarse, 0.0).astype(BF16)
 
-    cstrips[...] = dot(cpick_ref[:, pl.ds(0, plan.span)], coarse).astype(BF16)
+    cstrips[...] = dot(cpick_ref[:, pl.ds(0, 2 * plan.span)], coarse).astype(BF16)
     coarse_cols = pair(
         (
             (cstrips.at[pl.ds(0, plan.cstrip)], crecv.at[1]),
@@ -524,7 +556,7 @@
     copies["up_own"].wait()
     copies["up_side"].wait()
     copies["conv2"].wait()
-    up_sums = dot(up_own[:, pl.ds(0, plan.span)], coarse)
+    up_sums = dot(up_own[:, pl.ds(0, 2 * plan.span)], coarse)
     wait_recv_pair(coarse_cols)
     strips = jnp.concatenate([crecv[0], crecv[1]], axis=0)
     up_window[...] = (up_sums + dot(up_side[:, pl.ds(0, 2 * plan.cstrip)], strips)).astype(BF16)
@@ -561,9 +593,9 @@
     result = jnp.maximum(result, 0.0).reshape(plan.fr, width, wide)
     out_ref[...] = result[:, : plan.fc, :].astype(BF16)
 
-    for copy in feats + pool_copies + bp_copies + b_copies[0] + b_copies[1]:
+    for copy in feats[0] + feats[1] + pool_copies + bp_copies + b_copies[0] + b_copies[1]:
         copy.wait_send()
-    for made in sideways:
+    for made in sideways[0] + sideways[1]:
         for there, come, copy in made:
             @pl.when(there)
             def _():
@@ -590,7 +622,7 @@
     hidden_px = (plan.wr - 2) * plan.width
     feat_sends = 6 if rows == 4 else rows - 1
     scratch = [
-        pltpu.VMEM((plan.pixels, depth), BF16),
+        pltpu.VMEM((2, plan.pixels, depth), BF16),
         pltpu.VMEM((taps, 4 * own, depth), BF16),
         pltpu.VMEM((taps, depth, 4 * own), BF16),
         pltpu.VMEM((plan.fr * plan.fc, low_level.shape[2]), BF16),
@@ -600,13 +632,13 @@
         pltpu.VMEM(up_own.shape[1:], BF16),
         pltpu.VMEM(up_side.shape[1:], BF16),
         pltpu.VMEM(plan.low_window().shape, BF16),
-        pltpu.VMEM((3, plan.pixels, 4 * own), F32),
-        pltpu.VMEM((3, 2, plan.half, 2 * own), BF16),
-        pltpu.VMEM((3, 2, plan.half, 2 * own), BF16),
+        pltpu.VMEM((2, 3, plan.pixels, 4 * own), F32),
+        pltpu.VMEM((2, 3, 2, plan.half, 2 * own), BF16),
+        pltpu.VMEM((2, 3, 2, plan.half, 2 * own), BF16),
         pltpu.VMEM((cols, 8, own), F32),
         pltpu.VMEM((rows, 16, own), BF16),
-        pltpu.VMEM((2, rows, plan.span, 2 * own), BF16),
-        pltpu.VMEM((2, rows, plan.span, 2 * own), BF16),
+        pltpu.VMEM((2, rows, plan.span, 4 * own), BF16),
+        pltpu.VMEM((2, rows, plan.span, 4 * own), BF16),
         pltpu.VMEM((rows, 4 * own, out_width), BF16),
         pltpu.VMEM((2 * plan.cstrip, out_width), BF16),
         pltpu.VMEM((2, plan.cstrip, out_width), BF16),
@@ -617,9 +649,9 @@
         pltpu.VMEM((hidden_px, wide), F32),
         pltpu.VMEM((plan.window, out_width), BF16),
         pltpu.VMEM((hidden_px, wide), BF16),
-        dma((8 + 4 * taps,)),
-        dma((feat_sends,)), dma((feat_sends,)),
-        dma((3, 2)), dma((3, 2)),
+        dma((9 + 4 * taps,)),
+        dma((2, feat_sends)), dma((2, feat_sends)),
+        dma((2, 3, 2)), dma((2, 3, 2)),
         dma((cols - 1,)), dma((cols - 1,)),
         dma((rows - 1,)), dma((rows - 1,)),
         dma((2, rows - 1)), dma((2, rows - 1)),

time: 42.5 us -> 43 us (1.012)
  Pallas kernels: 40.7 us -> 41.2 us
    pallas_call x1, Pallas kernels: 40.7 us -> 41.2 us  [on_device(): pl.pallas_call(functools.partial(kernel, plan), out_shape=jax.ShapeDtypeS...]
where the time goes in v5:
time: 43 us; the launch traced here: 42.9 us
  Pallas kernels  41.2 us (96%)
  local copies, waits for them, and re-layouts  1.62 us (4%)
    pallas_call x1, Pallas kernels, on_device(): pl.pallas_call(functools.partial(kernel, plan), out_shape=jax.ShapeDtypeS...  41.2 us
    unnamed x1, local copies, waits for them, and re-layouts  1.62 us

profile of v5, /device:TPU:0, one launch (start us, length us, event | category | flops | bytes accessed | tf_op | source)
XLA Modules:
  0.0 42.9 jit_solution(15476923613688010133)
XLA Ops:
  0.0 41.2 %shard_map.190 = bf16[16,24,256]{2,1,0:T(8,128)(2,1)} custom-call(bf16[96,2048]{1,0:T(8,128)(2,1)} %bitcast.13, bf16[384,256]{1,0:T(8,128)(2,1)} %bitcast.16, bf16[64,2048]{1,0:T(8,128)(2,1)} %bitcast.14, bf16[3,3,3,64,2048]{4,3,2,1,0:T(8,128)(2,1)} %bitcast.12, bf16[64,2048]{1,0:T(8,128)(2,1)} %bitcast.15, f32[5,64]{1,0:T(8,128)} %aspp_bias_ref.1, ...), custom_call_target="tpu_custom_call" | custom-call | tf_op jit(solution)/shard_map/pallas_call | solution.py:660
  41.3 1.6 %copy.22 = bf16[16,24,256]{2,1,0:T(8,128)(2,1)} copy(bf16[16,24,256]{2,1,0:T(8,128)(2,1)} %shard_map.190) | data formatting | bytes 393216

commit v6 on v4

--- a/solution.py
+++ b/solution.py
@@ -293,11 +293,11 @@
 
     piece = min(256, depth)
 
-    def turn_weights():
-        for name, copy in copies.items():
-            if name[0] == "tap":
-                copy.wait()
-        for place in range(len(plan.taps)):
+    def turn_weights(places):
+        for place in places:
+            for name, copy in copies.items():
+                if name[:2] == ("tap", place):
+                    copy.wait()
             for begin in range(0, depth, piece):
                 turned[place, pl.ds(begin, piece), :] = weights[place, :, pl.ds(begin, piece)].T
 
@@ -341,8 +341,10 @@
     )
     start_pair(low_rows)
 
-    turn_weights()
+    middle = len(plan.taps) // 2
+    turn_weights(range(middle))
     pass_on()
+    turn_weights(range(middle, len(plan.taps)))
     wait_recv_pair(low_rows)
     lsend[...] = dot(lpick_ref[:, pl.ds(0, plan.low)], low_all[pl.ds(0, plan.low), :]).astype(BF16)
     low_cols = pair(
@@ -360,6 +362,111 @@
             proj_blocks[w, pl.ds(slot * own, own), :] = proj[
                 pl.ds(branch * joined + w * own, own), :
             ]
+
+    copies["feat"].wait()
+    for copy in feats[2 if passing else 0:]:
+        copy.wait_recv()
+
+    half = plan.half
+    sideways = [None, None, None]
+    pool_copies = []
+    for number in (2, 1, 0):
+        rate = RATES[number]
+        products(number)
+        for side in range(2):
+            lanes = pl.ds(side * own, own)
+            zsend[number, side] = jnp.concatenate(
+                [sums[number, pl.ds(0, half), lanes], sums[number, pl.ds(half, half), lanes]], axis=1
+            ).astype(BF16)
+        made = []
+        for side, far in ((0, distances[number]), (1, -distances[number])):
+            there = col + far < cols if far > 0 else col + far >= 0
+            come = col - far < cols if far < 0 else col - far >= 0
+            copy = pltpu.make_async_remote_copy(
+                src_ref=zsend.at[number, side], dst_ref=zrecv.at[number, side],
+                send_sem=z_send.at[number, side], recv_sem=z_recv.at[number, side],
+                device_id=(dp, row, lax.rem(col + far + 4 * cols, cols)), device_id_type=MESH,
+            )
+            made.append((there, come, copy))
+
+            @pl.when(there)
+            def _():
+                copy.start()
+        sideways[number] = made
+        if number == 1:
+            part = jnp.sum(sums[number, :, pl.ds(3 * own, own)], axis=0, keepdims=True)
+            pools[col] = jnp.broadcast_to(part, (8, own))
+            for step in range(1, cols):
+                copy = pltpu.make_async_remote_copy(
+                    src_ref=pools.at[col], dst_ref=pools.at[col],
+                    send_sem=pool_send.at[step - 1], recv_sem=pool_recv.at[step - 1],
+                    device_id=(dp, row, col_peer(step)), device_id_type=MESH,
+                )
+                copy.start()
+                pool_copies.append(copy)
+
+    def bias(number):
+        return aspp_bias_ref[pl.ds(number, 1), :]
+
+    def point_branch(part):
+        value = sums[0, pl.ds(part * half, half), pl.ds(3 * own, own)]
+        return jnp.maximum(value + bias(0), 0.0).astype(BF16)
+
+    def arrive(number):
+        for there, come, copy in sideways[number]:
+            @pl.when(come)
+            def _():
+                copy.wait_recv()
+
+    def atrous_branch(number, part):
+        lanes = pl.ds(part * own, own)
+        value = sums[number, pl.ds(part * half, half), pl.ds(2 * own, own)]
+        value = value + zrecv[number, 0, :, lanes].astype(F32) + zrecv[number, 1, :, lanes].astype(F32)
+        return jnp.maximum(value + bias(number + 1), 0.0).astype(BF16)
+
+    b_copies = [[], []]
+
+    def send_branches(message, made):
+        joint = [jnp.concatenate(made(part), axis=1) for part in range(2)]
+        joint = jnp.concatenate(joint, axis=0)
+        for place in range(rows):
+            value = joint[place * tile:(place + 1) * tile]
+            branches[message, place, pl.ds(plan.lead, tile), :] = value
+            ends = dot(rpick_ref[:, pl.ds(0, tile)], value).astype(BF16)
+            if place + 1 < rows:
+                branches[message, place + 1, pl.ds(0, plan.lead), :] = ends[: plan.lead]
+            if place > 0:
+                branches[message, place - 1, pl.ds(plan.lead + tile, plan.lead), :] = ends[plan.lead:]
+        for step in range(1, rows):
+            copy = pltpu.make_async_remote_copy(
+                src_ref=branches.at[message, row_peer(step)], dst_ref=brecv.at[message, row],
+                send_sem=b_send.at[message, step - 1], recv_sem=b_recv.at[message, step - 1],
+                device_id=(dp, row_peer(step), col), device_id_type=MESH,
+            )
+            copy.start()
+            b_copies[message].append(copy)
+        brecv[message, row] = branches[message, row]
+
+    arrive(2)
+    send_branches(0, lambda part: [point_branch(part), atrous_branch(2, part)])
+
+    for copy in pool_copies:
+        copy.wait_recv()
+    pooled = pools[0]
+    for place in range(1, cols):
+        pooled = pooled + pools[place]
+    pooled = pooled / (plan.height * cols * tc)
+    last = jnp.maximum(pooled + aspp_bias_ref[pl.ds(4, 1), :], 0.0)
+    branch_pool[row] = jnp.concatenate([last, last], axis=0).astype(BF16)
+    bp_copies = []
+    for step in range(1, rows):
+        copy = pltpu.make_async_remote_copy(
+            src_ref=branch_pool.at[row], dst_ref=branch_pool.at[row],
+            send_sem=bp_send.at[step - 1], recv_sem=bp_recv.at[step - 1],
+            device_id=(dp, row_peer(step), col), device_id_type=MESH,
+        )
+        copy.start()
+        bp_copies.append(copy)
 
     wait_recv_pair(low_cols)
     copies["lwindow"].wait()
@@ -385,111 +492,6 @@
         else:
             shifted[j - 1, pl.ds(0, hidden_px), :] = total
     low_part[...] += shifted[0, pl.ds(1, hidden_px), :] + shifted[1, pl.ds(2, hidden_px), :]
-
-    copies["feat"].wait()
-    for copy in feats[2 if passing else 0:]:
-        copy.wait_recv()
-
-    half = plan.half
-    sideways = [None, None, None]
-    pool_copies = []
-    for number in (2, 1, 0):
-        rate = RATES[number]
-        products(number)
-        for side in range(2):
-            lanes = pl.ds(side * own, own)
-            zsend[number, side] = jnp.concatenate(
-                [sums[number, pl.ds(0, half), lanes], sums[number, pl.ds(half, half), lanes]], axis=1
-            ).astype(BF16)
-        made = []
-        for side, far in ((0, distances[number]), (1, -distances[number])):
-            there = col + far < cols if far > 0 else col + far >= 0
-            come = col - far < cols if far < 0 else col - far >= 0
-            copy = pltpu.make_async_remote_copy(
-                src_ref=zsend.at[number, side], dst_ref=zrecv.at[number, side],
-                send_sem=z_send.at[number, side], recv_sem=z_recv.at[number, side],
-                device_id=(dp, row, lax.rem(col + far + 4 * cols, cols)), device_id_type=MESH,
-            )
-            made.append((there, come, copy))
-
-            @pl.when(there)
-            def _():
-                copy.start()
-        sideways[number] = made
-        if number == 1:
-            part = jnp.sum(sums[number, :, pl.ds(3 * own, own)], axis=0, keepdims=True)
-            pools[col] = jnp.broadcast_to(part, (8, own))
-            for step in range(1, cols):
-                copy = pltpu.make_async_remote_copy(
-                    src_ref=pools.at[col], dst_ref=pools.at[col],
-                    send_sem=pool_send.at[step - 1], recv_sem=pool_recv.at[step - 1],
-                    device_id=(dp, row, col_peer(step)), device_id_type=MESH,
-                )
-                copy.start()
-                pool_copies.append(copy)
-
-    def bias(number):
-        return aspp_bias_ref[pl.ds(number, 1), :]
-
-    def point_branch(part):
-        value = sums[0, pl.ds(part * half, half), pl.ds(3 * own, own)]
-        return jnp.maximum(value + bias(0), 0.0).astype(BF16)
-
-    def arrive(number):
-        for there, come, copy in sideways[number]:
-            @pl.when(come)
-            def _():
-                copy.wait_recv()
-
-    def atrous_branch(number, part):
-        lanes = pl.ds(part * own, own)
-        value = sums[number, pl.ds(part * half, half), pl.ds(2 * own, own)]
-        value = value + zrecv[number, 0, :, lanes].astype(F32) + zrecv[number, 1, :, lanes].astype(F32)
-        return jnp.maximum(value + bias(number + 1), 0.0).astype(BF16)
-
-    b_copies = [[], []]
-
-    def send_branches(message, made):
-        joint = [jnp.concatenate(made(part), axis=1) for part in range(2)]
-        joint = jnp.concatenate(joint, axis=0)
-        for place in range(rows):
-            value = joint[place * tile:(place + 1) * tile]
-            branches[message, place, pl.ds(plan.lead, tile), :] = value
-            ends = dot(rpick_ref[:, pl.ds(0, tile)], value).astype(BF16)
-            if place + 1 < rows:
-                branches[message, place + 1, pl.ds(0, plan.lead), :] = ends[: plan.lead]
-            if place > 0:
-                branches[message, place - 1, pl.ds(plan.lead + tile, plan.lead), :] = ends[plan.lead:]
-        for step in range(1, rows):
-            copy = pltpu.make_async_remote_copy(
-                src_ref=branches.at[message, row_peer(step)], dst_ref=brecv.at[message, row],
-                send_sem=b_send.at[message, step - 1], recv_sem=b_recv.at[message, step - 1],
-                device_id=(dp, row_peer(step), col), device_id_type=MESH,
-            )
-            copy.start()
-            b_copies[message].append(copy)
-        brecv[message, row] = branches[message, row]
-
-    arrive(2)
-    send_branches(0, lambda part: [point_branch(part), atrous_branch(2, part)])
-
-    for copy in pool_copies:
-        copy.wait_recv()
-    pooled = pools[0]
-    for place in range(1, cols):
-        pooled = pooled + pools[place]
-    pooled = pooled / (plan.height * cols * tc)
-    last = jnp.maximum(pooled + aspp_bias_ref[pl.ds(4, 1), :], 0.0)
-    branch_pool[row] = jnp.concatenate([last, last], axis=0).astype(BF16)
-    bp_copies = []
-    for step in range(1, rows):
-        copy = pltpu.make_async_remote_copy(
-            src_ref=branch_pool.at[row], dst_ref=branch_pool.at[row],
-            send_sem=bp_send.at[step - 1], recv_sem=bp_recv.at[step - 1],
-            device_id=(dp, row_peer(step), col), device_id_type=MESH,
-        )
-        copy.start()
-        bp_copies.append(copy)
 
     arrive(1)
     arrive(0)

time: 42.5 us -> 41.6 us (0.979)
  Pallas kernels: 40.7 us -> 39.9 us
    pallas_call x1, Pallas kernels: 40.7 us -> 39.9 us  [on_device(): pl.pallas_call(functools.partial(kernel, plan), out_shape=jax.ShapeDtypeS...]
where the time goes in v6:
time: 41.6 us; the launch traced here: 41.5 us
  Pallas kernels  39.9 us (96%)
  local copies, waits for them, and re-layouts  1.62 us (4%)
    pallas_call x1, Pallas kernels, on_device(): pl.pallas_call(functools.partial(kernel, plan), out_shape=jax.ShapeDtypeS...  39.9 us
    unnamed x1, local copies, waits for them, and re-layouts  1.62 us

profile of v6, /device:TPU:0, one launch (start us, length us, event | category | flops | bytes accessed | tf_op | source)
XLA Modules:
  0.0 41.5 jit_solution(1584819016501695378)
XLA Ops:
  0.0 39.9 %shard_map.190 = bf16[16,24,256]{2,1,0:T(8,128)(2,1)} custom-call(bf16[96,2048]{1,0:T(8,128)(2,1)} %bitcast.13, bf16[384,256]{1,0:T(8,128)(2,1)} %bitcast.16, bf16[64,2048]{1,0:T(8,128)(2,1)} %bitcast.14, bf16[3,3,3,64,2048]{4,3,2,1,0:T(8,128)(2,1)} %bitcast.12, bf16[64,2048]{1,0:T(8,128)(2,1)} %bitcast.15, f32[5,64]{1,0:T(8,128)} %aspp_bias_ref.1, ...), custom_call_target="tpu_custom_call" | custom-call | tf_op jit(solution)/shard_map/pallas_call | solution.py:630
  39.9 1.6 %copy.22 = bf16[16,24,256]{2,1,0:T(8,128)(2,1)} copy(bf16[16,24,256]{2,1,0:T(8,128)(2,1)} %shard_map.190) | data formatting | bytes 393216
